TPU v7x, 32 devices: a whole 2x2x4 slice. The times are simulated.
32 devices in a mesh: sector: 4 (over x, core), section: 8 (over z, y).
Axes of the slice: x: 2, y: 2, z: 4, core: 2. Of those that a mesh axis runs over, the one named last changes fastest.
Arguments:
- vectors: bfloat16 [12288, 512], P(('sector', 'section')), may hold values from -6 to 6
- sectors: int32 [12288, 2], P(('sector', 'section')), may hold values from 0 to 15, all different within a row; in each aligned block of 384 rows (0 to 383, 384 to 767, ...) at most 72 rows name the same one
- outcomes: int32 [12288, 2], P(('sector', 'section')), may hold values from 0 to 3
- sites: bfloat16 [2, 16, 512, 2048], P(None, 'sector'), may hold values from -0.25 to 0.25
- environments: bfloat16 [2, 16, 4, 512, 512], P(None, 'sector', None, 'section'), may hold values from -100 to 150, as said below
Outputs:
- probabilities: bfloat16 [12288, 8], P(('sector', 'section'))
- final_vectors: bfloat16 [12288, 512], P(('sector', 'section'))
Inputs may be any that keep to these rules, and one draw needn't show every extreme that they name: `sectors`: in the rows of one device no sector appears more than 72 times over all orbitals together, and on some device some sector appears exactly 72 times. Every block environments[k, q, s] is symmetric and positive definite.
All inputs are finite; a program needn't handle non-finite values.
Results may differ from a plain program's by a relative error of at most 0.0049.
Values may be sent and summed in bfloat16 or wider, within the bound.
A program may use at most 128 MiB of HBM per device.

v0:
```python
import jax
import jax.numpy as jnp
from jax import lax
from jax.sharding import PartitionSpec as P

OUTCOMES = 4
ORBITALS = 2


def slot_positions(labels, sector_total):
    onehot = (labels[:, None] == jnp.arange(sector_total, dtype=jnp.int32)[None, :]).astype(
        jnp.int32
    )
    before = jnp.cumsum(onehot, axis=0) - onehot
    return jnp.sum(before * onehot, axis=1)


def branch_results(amplitudes, images, id_grid, block_width):
    weights = jnp.sum(images * amplitudes, axis=-1)
    norm_sum = jnp.sum(weights, axis=-1)
    filled = id_grid >= 0.0
    branch_probs = (weights / jnp.where(filled, norm_sum, 1.0)[..., None]).astype(jnp.bfloat16)
    chosen_mask = (id_grid[..., None] == jnp.arange(OUTCOMES, dtype=jnp.float32)).astype(
        jnp.float32
    )
    chosen_weight = jnp.sum(chosen_mask * weights, axis=-1)
    picked = jnp.sum(chosen_mask[..., None] * amplitudes, axis=-2)
    rescale = lax.rsqrt(jnp.where(filled, chosen_weight, 1.0) / block_width)
    advanced = (picked * rescale[..., None]).astype(jnp.bfloat16)
    return (branch_probs, advanced)


def local(vectors, sectors, outcomes, sites, environments):
    sector_count = lax.axis_size("sector")
    per_device = sites.shape[1]
    sector_total = per_device * sector_count
    sample_count = vectors.shape[0]
    block_width = vectors.shape[1]
    capacity = max(2, (3 * sample_count + sector_total - 1) // sector_total)
    current = vectors
    columns = []
    for orbital in range(ORBITALS):
        environ_k = lax.all_gather(environments[orbital], "section", axis=2, tiled=True)
        site_k = sites[orbital]
        labels = sectors[:, orbital]
        slot_of = labels * capacity + slot_positions(labels, sector_total)
        send_rows = (
            jnp.zeros((sector_total * capacity, block_width), jnp.bfloat16).at[slot_of].set(current)
        )
        send_rows = send_rows.reshape(sector_total, capacity, block_width)
        send_ids = (
            jnp.full((sector_total * capacity,), -1.0, jnp.bfloat16)
            .at[slot_of]
            .set(outcomes[:, orbital].astype(jnp.bfloat16))
        )
        send_ids = send_ids.reshape(sector_total, capacity)
        rows_in = lax.all_to_all(send_rows, "sector", split_axis=0, concat_axis=0, tiled=True)
        ids_in = lax.all_to_all(send_ids, "sector", split_axis=0, concat_axis=0, tiled=True)
        slot_count = rows_in.shape[1]
        arranged = rows_in.reshape(sector_count, per_device, slot_count, block_width)
        amplitudes = jnp.einsum(
            "iqcb,qbf->iqcf", arranged, site_k, preferred_element_type=jnp.float32
        )
        amplitudes = amplitudes.reshape(sector_count, per_device, slot_count, OUTCOMES, block_width)
        rounded = amplitudes.astype(jnp.bfloat16)
        images = jnp.einsum(
            "iqcsb,qsbe->iqcse", rounded, environ_k, preferred_element_type=jnp.float32
        )
        id_grid = ids_in.astype(jnp.float32).reshape(sector_count, per_device, slot_count)
        branch_probs, advanced = branch_results(amplitudes, images, id_grid, block_width)
        probs_back, rows_back = (
            lax.all_to_all(
                branch_probs.reshape(sector_total, slot_count, OUTCOMES),
                "sector",
                split_axis=0,
                concat_axis=0,
                tiled=True,
            ),
            lax.all_to_all(
                advanced.reshape(sector_total, slot_count, block_width),
                "sector",
                split_axis=0,
                concat_axis=0,
                tiled=True,
            ),
        )
        columns.append(probs_back.reshape(sector_total * capacity, OUTCOMES)[slot_of])
        current = rows_back.reshape(sector_total * capacity, block_width)[slot_of]
    return (jnp.concatenate(columns, axis=1), current)


def solution(mesh):
    placed = (
        P(("sector", "section"), None),
        P(("sector", "section"), None),
        P(("sector", "section"), None),
        P(None, "sector", None, None),
        P(None, "sector", None, "section", None),
    )
    return jax.shard_map(
        local,
        mesh=mesh,
        in_specs=placed,
        out_specs=(P(("sector", "section"), None), P(("sector", "section"), None)),
        check_vma=False,
    )
```

profile of v0, /device:TPU:0, one launch (start us, length us, event | category | flops | bytes accessed | tf_op | source)
XLA Modules:
  0.0 311.3 jit_solution(9542134105820413448)
XLA Ops:
  16.1 4.2 %all-to-all-start.1 = ((bf16[4,4,72]{2,1,0:T(4,128)(2,1)}), bf16[4,4,72]{2,1,0:T(4,128)(2,1)S(1)}, u32[]{:S(2)}, u32[]{:S(2)}) async-start(bf16[4,4,72]{2,1,0:T(4,128)(2,1)} %all_to_all.31), calls=%async_computation.1 | async-start | bytes 8192 | tf_op jit(solution)/shard_map/all_to_all | solution.py:58
  20.3 3.6 %scatter_custom_fusion = bf16[1152,512]{1,0:T(8,128)(2,1)} fusion(s32[384]{0:T(512)S(1)} %get-tuple-element.10, bf16[384,512]{1,0:T(8,128)(2,1)} %param.5, bf16[]{:T(256)} %constant.9.clone.1), kind=kCustom, calls=%fused_computation.36 | custom fusion | bytes 1180160 | tf_op jit(solution)/shard_map/scatter | solution.py:48
  24.1 3.7 %all-to-all-start = ((bf16[16,72,512]{2,1,0:T(8,128)(2,1)}), bf16[16,72,512]{2,1,0:T(8,128)(2,1)S(1)}, u32[]{:S(2)}, u32[]{:S(2)}) async-start(bf16[16,72,512]{2,1,0:T(8,128)(2,1)} %bitcast.1), calls=%async_computation | async-start | bytes 2359296 | tf_op jit(solution)/shard_map/all_to_all | solution.py:57
  28.1 15.4 %all-to-all-done = bf16[16,72,512]{2,1,0:T(8,128)(2,1)S(1)} async-done(((bf16[16,72,512]{2,1,0:T(8,128)(2,1)}), bf16[16,72,512]{2,1,0:T(8,128)(2,1)S(1)}, u32[]{:S(2)}, u32[]{:S(2)}) %all-to-all-start) | async-done | bytes 1179680 | tf_op jit(solution)/shard_map/all_to_all | solution.py:57
  43.5 9.7 %fusion.6 = f32[4,4,72,2048]{3,2,1,0:T(8,128)} fusion(bf16[2,4,512,2048]{3,2,1,0:T(8,128)(2,1)} %param.8, bf16[4,4,72,512]{3,2,1,0:T(8,128)(2,1)S(1)} %bitcast.134), kind=kOutput, calls=%fused_computation.18 | convolution fusion | flops 2415919104 | bytes 19005440 | tf_op jit(solution)/shard_map/iqcb,qbf->iqcf/dot_general | solution.py:61
  53.2 12.3 %reshape.117 = f32[4,4,72,4,512]{4,3,2,0,1:T(4,128)} reshape(f32[4,4,72,2048]{3,2,0,1:T(8,128)} %bitcast.128) | data formatting | bytes 18874368 | tf_op jit(solution)/shard_map/reshape | solution.py:64
  65.5 28.9 %fusion.41 = (bf16[4,4,72,4,512]{4,3,2,0,1:T(4,128)(2,1)}, f32[4,4,72,512]{3,2,0,1:T(8,128)S(1)}) fusion(f32[4,4,72,4,512]{4,3,2,0,1:T(4,128)} %reshape.117, f32[4,4,72,4]{3,2,0,1:T(8,128)S(1)} %copy.87), kind=kLoop, calls=%fused_computation.88 | loop fusion | flops 6488064 | bytes 16533504 | tf_op jit(solution)/shard_map/convert_element_type | solution.py:65
  94.7 43.5 %all-gather.5.cloned.1.call-done = bf16[1,4,4,512,512]{4,3,2,1,0:T(8,128)(2,1)} async-done(((bf16[1,4,4,64,512]{4,3,2,1,0:T(8,128)(2,1)}), bf16[1,4,4,512,512]{4,3,2,1,0:T(8,128)(2,1)}) %all-gather.5.cloned.1.call-update) | async-done | bytes 8388624 | tf_op jit(solution)/shard_map/all_gather | solution.py:43
  138.2 10.8 %fusion.12 = (f32[4,4,72]{2,0,1:T(4,128)S(1)}, f32[4,4,72,4]{2,0,3,1:T(4,128)S(1)}) fusion(f32[4,4,9,4,8,512]{5,4,3,2,1,0:T(8,128)} %bitcast.129, bf16[1,4,4,512,512]{4,3,2,1,0:T(8,128)(2,1)} %all-gather.5.cloned.1.call-done, bf16[4,4,72,4,512]{4,3,2,0,1:T(4,128)(2,1)} %get-tuple-element.16), kind=kOutput, calls=%fused_computation.24 | convolution fusion | flops 2422991360 | bytes 22567424 | tf_op jit(solution)/shard_map/iqcsb,qsbe->iqcse/dot_general | solution.py:66
  150.3 3.7 %all-to-all-start.3 = ((bf16[16,72,512]{2,1,0:T(8,128)(2,1)}), bf16[16,72,512]{2,1,0:T(8,128)(2,1)S(1)}, u32[]{:S(2)}, u32[]{:S(2)}) async-start(bf16[16,72,512]{2,1,0:T(8,128)(2,1)} %fusion.17), calls=%async_computation.3 | async-start | bytes 2359296 | tf_op jit(solution)/shard_map/all_to_all | solution.py:79
  159.0 10.7 %all-to-all-done.3 = bf16[16,72,512]{2,1,0:T(8,128)(2,1)S(1)} async-done(((bf16[16,72,512]{2,1,0:T(8,128)(2,1)}), bf16[16,72,512]{2,1,0:T(8,128)(2,1)S(1)}, u32[]{:S(2)}, u32[]{:S(2)}) %all-to-all-start.3) | async-done | bytes 1179680 | tf_op jit(solution)/shard_map/all_to_all | solution.py:79
  169.7 3.2 %all-to-all-start.5 = ((bf16[4,4,72]{2,1,0:T(4,128)(2,1)}), bf16[4,4,72]{2,1,0:T(4,128)(2,1)S(1)}, u32[]{:S(2)}, u32[]{:S(2)}) async-start(bf16[4,4,72]{2,1,0:T(4,128)(2,1)} %all_to_all.36), calls=%async_computation.5 | async-start | bytes 8192 | tf_op jit(solution)/shard_map/all_to_all | solution.py:58
  173.0 4.8 %scatter_custom_fusion.2 = bf16[1152,512]{1,0:T(8,128)(2,1)} fusion(s32[384]{0:T(512)S(1)} %fusion.40, bf16[]{:T(256)} %constant.9.clone.1, bf16[1152,512]{1,0:T(8,128)(2,1)S(1)} %bitcast.137, s32[1024]{0:T(1024)S(1)} %pad_clamp_fusion.1), kind=kCustom, calls=%fused_computation.34 | custom fusion | bytes 1179650 | tf_op jit(solution)/shard_map/scatter | solution.py:48
  177.8 3.5 %all-to-all-start.4 = ((bf16[16,72,512]{2,1,0:T(8,128)(2,1)}), bf16[16,72,512]{2,1,0:T(8,128)(2,1)S(1)}, u32[]{:S(2)}, u32[]{:S(2)}) async-start(bf16[16,72,512]{2,1,0:T(8,128)(2,1)} %bitcast.18), calls=%async_computation.4 | async-start | bytes 2359296 | tf_op jit(solution)/shard_map/all_to_all | solution.py:57
  182.3 14.9 %all-to-all-done.4 = bf16[16,72,512]{2,1,0:T(8,128)(2,1)S(1)} async-done(((bf16[16,72,512]{2,1,0:T(8,128)(2,1)}), bf16[16,72,512]{2,1,0:T(8,128)(2,1)S(1)}, u32[]{:S(2)}, u32[]{:S(2)}) %all-to-all-start.4) | async-done | bytes 1179680 | tf_op jit(solution)/shard_map/all_to_all | solution.py:57
  197.2 3.5 %all-to-all-start.2 = ((bf16[16,72,4]{1,2,0:T(4,128)(2,1)}), bf16[16,72,4]{1,2,0:T(4,128)(2,1)S(1)}, u32[]{:S(2)}, u32[]{:S(2)}) async-start(bf16[16,72,4]{1,2,0:T(4,128)(2,1)} %copy.84), calls=%async_computation.2 | async-start | bytes 32768 | tf_op jit(solution)/shard_map/all_to_all | solution.py:72
  200.7 9.6 %fusion.2 = f32[4,4,72,2048]{3,2,1,0:T(8,128)} fusion(bf16[2,4,512,2048]{3,2,1,0:T(8,128)(2,1)} %param.8, bf16[4,4,72,512]{3,2,1,0:T(8,128)(2,1)S(1)} %bitcast.133), kind=kOutput, calls=%fused_computation.14 | convolution fusion | flops 2415919104 | bytes 19005440 | tf_op jit(solution)/shard_map/iqcb,qbf->iqcf/dot_general | solution.py:61
  210.3 12.4 %reshape.123 = f32[4,4,72,4,512]{4,3,2,0,1:T(4,128)} reshape(f32[4,4,72,2048]{3,2,0,1:T(8,128)} %bitcast.130) | data formatting | bytes 18874368 | tf_op jit(solution)/shard_map/reshape | solution.py:64
  222.7 14.8 %multiply_reduce_fusion = (f32[4,4,72,512]{3,2,0,1:T(8,128)}, bf16[4,4,72,4,512]{4,3,2,0,1:T(4,128)(2,1)}) fusion(f32[4,4,72,4,512]{4,3,2,0,1:T(4,128)} %reshape.123, f32[4,4,72,4]{3,2,0,1:T(8,128)S(1)} %copy.101), kind=kLoop, calls=%fused_computation.10 | loop fusion | flops 6488064 | bytes 16533504 | tf_op jit(solution)/shard_map/reduce_sum | solution.py:27
  237.5 26.0 %all-gather.7.cloned.1.call-done = bf16[1,4,4,512,512]{4,3,2,1,0:T(8,128)(2,1)} async-done(((bf16[1,4,4,64,512]{4,3,2,1,0:T(8,128)(2,1)}), bf16[1,4,4,512,512]{4,3,2,1,0:T(8,128)(2,1)}) %all-gather.7.cloned.1.call-update) | async-done | bytes 8388624 | tf_op jit(solution)/shard_map/all_gather | solution.py:43
  263.5 11.0 %fusion.14 = (f32[4,4,72]{2,0,1:T(4,128)S(1)}, f32[4,4,72,4]{2,0,3,1:T(4,128)S(1)}) fusion(f32[4,4,9,4,8,512]{5,4,3,2,1,0:T(8,128)} %bitcast.131, bf16[1,4,4,512,512]{4,3,2,1,0:T(8,128)(2,1)} %all-gather.7.cloned.1.call-done, bf16[4,4,72,4,512]{4,3,2,0,1:T(4,128)(2,1)} %get-tuple-element.15), kind=kOutput, calls=%fused_computation.26 | convolution fusion | flops 2422991360 | bytes 22567424 | tf_op jit(solution)/shard_map/iqcsb,qsbe->iqcse/dot_general | solution.py:66
  275.5 3.3 %all-to-all-start.6 = ((bf16[16,72,4]{1,2,0:T(4,128)(2,1)}), bf16[16,72,4]{1,2,0:T(4,128)(2,1)S(1)}, u32[]{:S(2)}, u32[]{:S(2)}) async-start(bf16[16,72,4]{1,2,0:T(4,128)(2,1)} %copy.97), calls=%async_computation.6 | async-start | bytes 32768 | tf_op jit(solution)/shard_map/all_to_all | solution.py:72
  282.6 3.5 %all-to-all-start.7 = ((bf16[16,72,512]{2,1,0:T(8,128)(2,1)}), bf16[16,72,512]{2,1,0:T(8,128)(2,1)S(1)}, u32[]{:S(2)}, u32[]{:S(2)}) async-start(bf16[16,72,512]{2,1,0:T(8,128)(2,1)} %fusion.16), calls=%async_computation.7 | async-start | bytes 2359296 | tf_op jit(solution)/shard_map/all_to_all | solution.py:79
  290.3 11.6 %all-to-all-done.7 = bf16[16,72,512]{2,1,0:T(8,128)(2,1)S(1)} async-done(((bf16[16,72,512]{2,1,0:T(8,128)(2,1)}), bf16[16,72,512]{2,1,0:T(8,128)(2,1)S(1)}, u32[]{:S(2)}, u32[]{:S(2)}) %all-to-all-start.7) | async-done | bytes 1179680 | tf_op jit(solution)/shard_map/all_to_all | solution.py:79
  (68 shorter events, 28.2 us)
Async XLA Ops:
  7.2 4.0 %copy-start.1 = (s32[384,2]{0,1:T(2,128)S(1)}, s32[384,2]{0,1:T(2,128)}, u32[]{:S(2)}) copy-start(s32[384,2]{0,1:T(2,128)} %param.6) | copy-start | bytes 9220
  7.2 5.1 %copy-start.2 = (s32[384,2]{0,1:T(2,128)S(1)}, s32[384,2]{0,1:T(2,128)}, u32[]{:S(2)}) copy-start(s32[384,2]{0,1:T(2,128)} %param.7) | copy-start | bytes 9220
  7.2 131.0 %all-gather.5.cloned.1.call-start = ((), (), s32[]{:S(2)}) async-start(), calls=%async_computation.8 | async-start | bytes 9437184 | tf_op jit(solution)/shard_map/all_gather | solution.py:43
  10.4 253.1 %all-gather.7.cloned.1.call-start = ((), (), s32[]{:S(2)}) async-start(), calls=%async_computation.9 | async-start | bytes 9437184 | tf_op jit(solution)/shard_map/all_gather | solution.py:43
  16.1 8.0 %all-to-all-start.1 = ((bf16[4,4,72]{2,1,0:T(4,128)(2,1)}), bf16[4,4,72]{2,1,0:T(4,128)(2,1)S(1)}, u32[]{:S(2)}, u32[]{:S(2)}) async-start(bf16[4,4,72]{2,1,0:T(4,128)(2,1)} %all_to_all.31), calls=%async_computation.1 | async-start | bytes 8192 | tf_op jit(solution)/shard_map/all_to_all | solution.py:58
  24.1 19.4 %all-to-all-start = ((bf16[16,72,512]{2,1,0:T(8,128)(2,1)}), bf16[16,72,512]{2,1,0:T(8,128)(2,1)S(1)}, u32[]{:S(2)}, u32[]{:S(2)}) async-start(bf16[16,72,512]{2,1,0:T(8,128)(2,1)} %bitcast.1), calls=%async_computation | async-start | bytes 2359296 | tf_op jit(solution)/shard_map/all_to_all | solution.py:57
  150.3 19.4 %all-to-all-start.3 = ((bf16[16,72,512]{2,1,0:T(8,128)(2,1)}), bf16[16,72,512]{2,1,0:T(8,128)(2,1)S(1)}, u32[]{:S(2)}, u32[]{:S(2)}) async-start(bf16[16,72,512]{2,1,0:T(8,128)(2,1)} %fusion.17), calls=%async_computation.3 | async-start | bytes 2359296 | tf_op jit(solution)/shard_map/all_to_all | solution.py:79
  169.7 8.1 %all-to-all-start.5 = ((bf16[4,4,72]{2,1,0:T(4,128)(2,1)}), bf16[4,4,72]{2,1,0:T(4,128)(2,1)S(1)}, u32[]{:S(2)}, u32[]{:S(2)}) async-start(bf16[4,4,72]{2,1,0:T(4,128)(2,1)} %all_to_all.36), calls=%async_computation.5 | async-start | bytes 8192 | tf_op jit(solution)/shard_map/all_to_all | solution.py:58
  177.8 19.4 %all-to-all-start.4 = ((bf16[16,72,512]{2,1,0:T(8,128)(2,1)}), bf16[16,72,512]{2,1,0:T(8,128)(2,1)S(1)}, u32[]{:S(2)}, u32[]{:S(2)}) async-start(bf16[16,72,512]{2,1,0:T(8,128)(2,1)} %bitcast.18), calls=%async_computation.4 | async-start | bytes 2359296 | tf_op jit(solution)/shard_map/all_to_all | solution.py:57
  197.2 78.3 %all-to-all-start.2 = ((bf16[16,72,4]{1,2,0:T(4,128)(2,1)}), bf16[16,72,4]{1,2,0:T(4,128)(2,1)S(1)}, u32[]{:S(2)}, u32[]{:S(2)}) async-start(bf16[16,72,4]{1,2,0:T(4,128)(2,1)} %copy.84), calls=%async_computation.2 | async-start | bytes 32768 | tf_op jit(solution)/shard_map/all_to_all | solution.py:72
  263.5 11.1 %copy-start = (f32[4,4,72,512]{3,2,0,1:T(8,128)S(1)}, f32[4,4,72,512]{3,2,0,1:T(8,128)}, u32[]{:S(2)}) copy-start(f32[4,4,72,512]{3,2,0,1:T(8,128)} %get-tuple-element.14) | copy-start | bytes 7077892
  275.5 7.1 %all-to-all-start.6 = ((bf16[16,72,4]{1,2,0:T(4,128)(2,1)}), bf16[16,72,4]{1,2,0:T(4,128)(2,1)S(1)}, u32[]{:S(2)}, u32[]{:S(2)}) async-start(bf16[16,72,4]{1,2,0:T(4,128)(2,1)} %copy.97), calls=%async_computation.6 | async-start | bytes 32768 | tf_op jit(solution)/shard_map/all_to_all | solution.py:72
  282.6 19.4 %all-to-all-start.7 = ((bf16[16,72,512]{2,1,0:T(8,128)(2,1)}), bf16[16,72,512]{2,1,0:T(8,128)(2,1)S(1)}, u32[]{:S(2)}, u32[]{:S(2)}) async-start(bf16[16,72,512]{2,1,0:T(8,128)(2,1)} %fusion.16), calls=%async_computation.7 | async-start | bytes 2359296 | tf_op jit(solution)/shard_map/all_to_all | solution.py:79
Sparse Core Ops, SparseCore 0:
  10.5 127.6 all-gather.4
  140.4 123.0 all-gather.6
where the time goes:
time: 313 us; the launch traced here: 311 us
  waiting for transfers between devices  126 us (40%)
  local copies, waits for them, and re-layouts  52.5 us (17%)
  other arithmetic  49 us (16%)
  matrix products  41.1 us (13%)
  starting transfers between devices  28.8 us (9%)
  between operations  14.4 us (5%)
    all_gather x2, waiting for transfers between devices, local(): lax.all_gather(environments[orbital], 'section', axis=2, tiled=True)  69.5 us
    all_to_all x2, waiting for transfers between devices, local(): lax.all_to_all(send_rows, 'sector', split_axis=0, concat_axis=0, tiled=True)  30.3 us
    convert_element_type x1, other arithmetic, local(): rounded = amplitudes.astype(jnp.bfloat16)  28.9 us
    reshape x2, local copies, waits for them, and re-layouts, local(): amplitudes.reshape(sector_count, per_device, slot_count, OUTCOMES, block_...  24.7 us
    all_to_all x2, waiting for transfers between devices, local(): lax.all_to_all(advanced.reshape(sector_total, slot_count, block_width), '...  22.3 us
    dot_general x2, matrix products, local(): jnp.einsum('iqcsb,qsbe->iqcse', rounded, environ_k, preferred_element_typ...  21.8 us
    dot_general x2, matrix products, local(): jnp.einsum('iqcb,qbf->iqcf', arranged, site_k, preferred_element_type=jnp...  19.3 us
    reduce_sum x1, other arithmetic, branch_results(): picked = jnp.sum(chosen_mask[..., None] * amplitudes, axis=-2)  14.8 us
  transfers between devices with their start and end apart: 10, of which 8 were waited for; matrix products, arithmetic and copies ran while one was open for 44% of the time, Pallas kernels for 0%

commit v1 on v0

v1 whole, which is shorter than its diff:
```python
import jax
import jax.numpy as jnp
from jax import lax
from jax.sharding import Mesh, PartitionSpec as P

OUTCOMES = 4
ORBITALS = 2


def slot_positions(labels, sector_total):
    onehot = (labels[:, None] == jnp.arange(sector_total, dtype=jnp.int32)[None, :]).astype(
        jnp.bfloat16
    )
    count = labels.shape[0]
    lower = (jnp.arange(count)[:, None] > jnp.arange(count)[None, :]).astype(jnp.bfloat16)
    before = jnp.dot(lower, onehot, preferred_element_type=jnp.float32)
    return jnp.sum(before * onehot.astype(jnp.float32), axis=1).astype(jnp.int32)


def local(vectors, sectors, outcomes, sites, environments):
    per_device = sites.shape[1]
    sector_total = per_device * lax.axis_size("sector")
    sample_count, width = vectors.shape
    capacity = max(2, (3 * sample_count + sector_total - 1) // sector_total)
    slots = sector_total * capacity
    own = lax.axis_index("own")
    peers = ("sector", "own")

    environ = []
    for k in range(ORBITALS):
        part = lax.all_to_all(environments[k], "own", split_axis=0, concat_axis=0, tiled=True)
        whole = lax.all_gather(part, "grp", axis=0, tiled=True)
        whole = jnp.transpose(whole, (1, 0, 2, 3)).reshape(OUTCOMES, width, width)
        environ.append(whole)

    hots = []
    ids = []
    for k in range(ORBITALS):
        labels = sectors[:, k]
        slot_of = labels * capacity + slot_positions(labels, sector_total)
        hot = (jnp.arange(slots, dtype=jnp.int32)[:, None] == slot_of[None, :])
        hots.append(hot.astype(jnp.bfloat16))
        ids.append(jnp.sum(jnp.where(hot, outcomes[:, k][None, :] + 1, 0), axis=1) - 1)
    send_ids = jnp.stack(ids, 0).reshape(ORBITALS, sector_total, capacity).transpose(1, 0, 2)
    ids_in = lax.all_to_all(send_ids.astype(jnp.bfloat16), peers, split_axis=0, concat_axis=0, tiled=True)
    ids_in = ids_in.astype(jnp.float32)

    current = vectors
    probs_out = []
    for k in range(ORBITALS):
        hot = hots[k]
        rows = jnp.dot(hot, current, preferred_element_type=jnp.float32).astype(jnp.bfloat16)
        rows = rows.reshape(sector_total, capacity, width)
        rows_in = lax.all_to_all(rows, peers, split_axis=0, concat_axis=0, tiled=True)
        rows_in = rows_in.reshape(slots, width)
        site = lax.dynamic_index_in_dim(sites[k], own, 0, keepdims=False)
        chosen = ids_in[:, k, :].reshape(slots)
        weights = []
        picked = jnp.zeros((slots, width), jnp.float32)
        for s in range(OUTCOMES):
            amp = jnp.dot(rows_in, site[:, s * width : (s + 1) * width], preferred_element_type=jnp.float32)
            image = jnp.dot(amp.astype(jnp.bfloat16), environ[k][s], preferred_element_type=jnp.float32)
            weights.append(jnp.sum(image * amp, axis=-1))
            picked = jnp.where((chosen == s)[:, None], amp, picked)
        filled = chosen >= 0.0
        weights = jnp.stack(weights, 0)
        total = jnp.sum(weights, axis=0)
        probs = (weights / jnp.where(filled, total, 1.0)[None, :]).astype(jnp.bfloat16)
        probs_out.append(jnp.where(filled[None, :], probs, 0))
        mask = chosen[None, :] == jnp.arange(OUTCOMES, dtype=jnp.float32)[:, None]
        weight = jnp.sum(jnp.where(mask, weights, 0.0), axis=0)
        scale = lax.rsqrt(jnp.where(filled, weight, 1.0) / width)
        advanced = (picked * scale[:, None]).astype(jnp.bfloat16)
        back = lax.all_to_all(
            advanced.reshape(sector_total, capacity, width), peers, split_axis=0, concat_axis=0, tiled=True
        ).reshape(slots, width)
        current = lax.dot_general(
            hot, back, (((0,), (0,)), ((), ())), preferred_element_type=jnp.float32
        ).astype(jnp.bfloat16)
    probs = jnp.stack(probs_out, 0).reshape(ORBITALS * OUTCOMES, sector_total, capacity)
    probs = lax.all_to_all(probs.transpose(1, 0, 2), peers, split_axis=0, concat_axis=0, tiled=True)
    probs = probs.transpose(0, 2, 1).reshape(slots, ORBITALS, OUTCOMES)
    columns = []
    for k in range(ORBITALS):
        columns.append(
            lax.dot_general(hots[k], probs[:, k], (((0,), (0,)), ((), ())), preferred_element_type=jnp.float32)
        )
    return jnp.concatenate(columns, axis=1).astype(jnp.bfloat16), current


def solution(mesh):
    def run(vectors, sectors, outcomes, sites, environments):
        sector_size, section_size = mesh.devices.shape
        owners = sites.shape[1] // sector_size
        split = Mesh(
            mesh.devices.reshape(sector_size, section_size // owners, owners), ("sector", "grp", "own")
        )
        every = P(("sector", "grp", "own"), None)
        return jax.shard_map(
            local,
            mesh=split,
            in_specs=(
                every,
                every,
                every,
                P(None, "sector", None, None),
                P(None, "sector", None, ("grp", "own"), None),
            ),
            out_specs=(every, every),
            check_vma=False,
        )(vectors, sectors, outcomes, sites, environments)

    return run
```

time: 313 us -> 232 us (0.74)
  other arithmetic: 49 us -> 9.91 us
  local copies, waits for them, and re-layouts: 52.5 us -> 31.4 us
  waiting for transfers between devices: 126 us -> 112 us
  matrix products: 41.1 us -> 29.7 us
  starting transfers between devices: 28.8 us -> 33.2 us
    reshape x2, local copies, waits for them, and re-layouts: 24.7 us -> 0.21 us  [the longest x1 0.11 us: local(): probs = probs.transpose(0, 2, 1).reshape(slots, ORBITALS, OUTCOMES)]
    convert_element_type x11 -> x4, other arithmetic: 31.5 us -> 7.74 us  [the longest x2 7.72 us: local(): advanced = (picked * scale[:, None]).astype(jnp.bfloat16)]
    reduce_sum x5 -> x4, other arithmetic: 15 us -> 0.62 us  [the longest x2 0.54 us: local(): jnp.sum(jnp.where(hot, outcomes[:, k][None, :] + 1, 0), axis=1) - 1]
    scatter x4 -> x0, local copies, waits for them, and re-layouts: 14.4 us -> none  [the longest x2 8.44 us: local(): jnp.zeros((sector_total * capacity, block_width), jnp.bfloat16).at[slot_of]]
    slice x4 -> x5, local copies, waits for them, and re-layouts: 3.39 us -> 17.2 us  [the longest x1 12 us: local(): site = lax.dynamic_index_in_dim(sites[k], own, 0, keepdims=False)]
    dot_general x4 -> x23, matrix products: 41.1 us -> 29.7 us  [the longest x8 15.7 us: local(): jnp.dot(rows_in, site[:, s * width:(s + 1) * width], preferred_element_ty...]
    all_gather x2, waiting for transfers between devices: 69.5 us -> 59.3 us  [local(): whole = lax.all_gather(part, 'grp', axis=0, tiled=True)]
    squeeze x0 -> x3, local copies, waits for them, and re-layouts: none -> 9.63 us  [the longest x2 6.5 us: local(): site = lax.dynamic_index_in_dim(sites[k], own, 0, keepdims=False)]
  transfers between devices with their start and end apart: 10 -> 10, of which waited for: 8 -> 8; matrix products, arithmetic and copies ran while one was open for 44% -> 23% of each run, Pallas kernels for 0% -> 0%
where the time goes in v1:
time: 232 us; the launch traced here: 230 us
  waiting for transfers between devices  112 us (48%)
  starting transfers between devices  33.2 us (14%)
  local copies, waits for them, and re-layouts  31.4 us (14%)
  matrix products  29.7 us (13%)
  between operations  14.6 us (6%)
  other arithmetic  9.91 us (4%)
    all_gather x2, waiting for transfers between devices, local(): whole = lax.all_gather(part, 'grp', axis=0, tiled=True)  59.3 us
    all_to_all x2, waiting for transfers between devices, local(): lax.all_to_all(advanced.reshape(sector_total, capacity, width), peers, sp...  34.4 us
    dot_general x8, matrix products, local(): jnp.dot(rows_in, site[:, s * width:(s + 1) * width], preferred_element_ty...  15.7 us
    slice x1, local copies, waits for them, and re-layouts, local(): site = lax.dynamic_index_in_dim(sites[k], own, 0, keepdims=False)  12 us
    all_to_all x2, waiting for transfers between devices, local(): lax.all_to_all(environments[k], 'own', split_axis=0, concat_axis=0, tiled...  12 us
    all_to_all x2, starting transfers between devices, local(): lax.all_to_all(advanced.reshape(sector_total, capacity, width), peers, sp...  8.5 us
    convert_element_type x2, other arithmetic, local(): advanced = (picked * scale[:, None]).astype(jnp.bfloat16)  7.72 us
    all_to_all x2, starting transfers between devices, local(): lax.all_to_all(rows, peers, split_axis=0, concat_axis=0, tiled=True)  7.58 us
  transfers between devices with their start and end apart: 10, of which 8 were waited for; matrix products, arithmetic and copies ran while one was open for 23% of the time, Pallas kernels for 0%

profile of v1, /device:TPU:0, one launch (start us, length us, event | category | flops | bytes accessed | tf_op | source)
XLA Modules:
  0.0 230.3 jit_solution(5644616808637090945)
XLA Ops:
  10.5 6.3 %all-to-all-start = ((bf16[16,2,72]{2,1,0:T(2,128)(2,1)}), bf16[16,2,72]{2,1,0:T(2,128)(2,1)S(1)}, u32[]{:S(2)}, u32[]{:S(2)}) async-start(bf16[16,2,72]{2,1,0:T(2,128)(2,1)} %copy.34), calls=%async_computation | async-start | bytes 16384 | tf_op jit(solution)/shard_map/all_to_all | solution.py:45
  16.8 3.1 %slice_bitcast_fusion = (bf16[4,4,64,512]{3,2,1,0:T(8,128)(2,1)}, bf16[4,4,64,512]{3,2,1,0:T(8,128)(2,1)}) fusion(bf16[2,4,4,64,512]{4,3,2,1,0:T(8,128)(2,1)} %param.9), kind=kLoop, calls=%fused_computation.46 | loop fusion | bytes 4194304 | tf_op jit(solution)/shard_map/squeeze | solution.py:31
  20.0 2.3 all-to-all-done
  22.2 3.5 %all-to-all-start.2 = ((bf16[4,4,64,512]{3,2,1,0:T(8,128)(2,1)}), bf16[4,4,64,512]{3,2,1,0:T(8,128)(2,1)S(1)}, u32[]{:S(2)}, u32[]{:S(2)}) async-start(bf16[4,4,64,512]{3,2,1,0:T(8,128)(2,1)} %get-tuple-element.19), calls=%async_computation.2 | async-start | bytes 2097152 | tf_op jit(solution)/shard_map/all_to_all | solution.py:31
  27.6 12.0 %all-to-all-done.2 = bf16[4,4,64,512]{3,2,1,0:T(8,128)(2,1)S(1)} async-done(((bf16[4,4,64,512]{3,2,1,0:T(8,128)(2,1)}), bf16[4,4,64,512]{3,2,1,0:T(8,128)(2,1)S(1)}, u32[]{:S(2)}, u32[]{:S(2)}) %all-to-all-start.2) | async-done | bytes 1048608 | tf_op jit(solution)/shard_map/all_to_all | solution.py:31
  39.6 3.7 %all-to-all-start.1 = ((bf16[16,72,512]{2,1,0:T(8,128)(2,1)}), bf16[16,72,512]{2,1,0:T(8,128)(2,1)S(1)}, u32[]{:S(2)}, u32[]{:S(2)}) async-start(bf16[16,72,512]{2,1,0:T(8,128)(2,1)} %bitcast.68), calls=%async_computation.1 | async-start | bytes 2359296 | tf_op jit(solution)/shard_map/all_to_all | solution.py:54
  44.1 12.0 %fusion.57 = (bf16[1,4,512,2048]{3,2,1,0:T(8,128)(2,1)}, bf16[1,4,512,2048]{3,2,1,0:T(8,128)(2,1)}) fusion(bf16[2,4,512,2048]{3,2,1,0:T(8,128)(2,1)} %param.8), kind=kLoop, calls=%fused_computation.118 | loop fusion | bytes 33554432 | tf_op jit(solution)/shard_map/slice | solution.py:56
  56.1 3.4 %dynamic-slice_bitcast_fusion.1 = bf16[512,2048]{1,0:T(8,128)(2,1)} fusion(bf16[1,4,512,2048]{3,2,1,0:T(8,128)(2,1)} %get-tuple-element.13, s32[]{:T(128)S(6)} %select_n.96), kind=kLoop, calls=%fused_computation.13 | loop fusion | bytes 4194308 | tf_op jit(solution)/shard_map/jit(dynamic_index_in_dim)/squeeze | solution.py:56
  61.5 3.5 %all-to-all-start.5 = ((bf16[4,4,64,512]{3,2,1,0:T(8,128)(2,1)}), bf16[4,4,64,512]{3,2,1,0:T(8,128)(2,1)S(1)}, u32[]{:S(2)}, u32[]{:S(2)}) async-start(bf16[4,4,64,512]{3,2,1,0:T(8,128)(2,1)} %get-tuple-element.18), calls=%async_computation.5 | async-start | bytes 2097152 | tf_op jit(solution)/shard_map/all_to_all | solution.py:31
  65.0 3.4 %fusion.47 = f32[1152,512]{1,0:T(8,128)} fusion(bf16[1152,512]{1,0:T(8,128)(2,1)S(1)} %bitcast.57, bf16[512,2048]{1,0:T(8,128)(2,1)} %dynamic-slice_bitcast_fusion.1), kind=kOutput, calls=%fused_computation.69 | convolution fusion | flops 603979776 | bytes 4063232 | tf_op jit(solution)/shard_map/dot_general | solution.py:61
  75.0 28.8 %all-gather.3.cloned.1.call-done = bf16[8,4,64,512]{3,2,1,0:T(8,128)(2,1)} async-done(((bf16[4,4,64,512]{3,2,1,0:T(8,128)(2,1)}), bf16[8,4,64,512]{3,2,1,0:T(8,128)(2,1)}) %all-gather.3.cloned.1.call-update) | async-done | bytes 2097168 | tf_op jit(solution)/shard_map/all_gather | solution.py:32
  111.0 2.5 %multiply_convert_fusion.1 = bf16[1152,512]{1,0:T(8,128)(2,1)} fusion(f32[1152,512]{1,0:T(8,128)S(1)} %copy-done.10, f32[1152,512]{1,0:T(8,128)S(1)} %copy-done.9, f32[1152,512]{1,0:T(8,128)S(1)} %copy-done.8, f32[1152,512]{1,0:T(8,128)S(1)} %copy-done.7, f32[1152]{0:T(1024)S(1)} %multiply_rsqrt_fusion.1, pred[1152]{0:T(1024)(128)(4,1)S(1)} %get-tuple-element.29, ...), kind=kLoop, calls=%fused_computation.11 | loop fusion | flops 3538944 | bytes 10626048 | tf_op jit(solution)/shard_map/convert_element_type | solution.py:73
  113.6 3.8 %all-to-all-start.3 = ((bf16[16,72,512]{2,1,0:T(8,128)(2,1)}), bf16[16,72,512]{2,1,0:T(8,128)(2,1)S(1)}, u32[]{:S(2)}, u32[]{:S(2)}) async-start(bf16[16,72,512]{2,1,0:T(8,128)(2,1)} %bitcast.10), calls=%async_computation.3 | async-start | bytes 2359296 | tf_op jit(solution)/shard_map/all_to_all | solution.py:74
  118.1 18.4 %all-to-all-done.3 = bf16[16,72,512]{2,1,0:T(8,128)(2,1)S(1)} async-done(((bf16[16,72,512]{2,1,0:T(8,128)(2,1)}), bf16[16,72,512]{2,1,0:T(8,128)(2,1)S(1)}, u32[]{:S(2)}, u32[]{:S(2)}) %all-to-all-start.3) | async-done | bytes 1179680 | tf_op jit(solution)/shard_map/all_to_all | solution.py:74
  136.5 2.5 %convolution_convert_fusion = bf16[1152,512]{1,0:T(8,128)(2,1)} fusion(bf16[1152,512]{1,0:T(8,128)(2,1)S(1)} %bitcast.70, s32[384]{0:T(512)S(1)} %get-tuple-element.32, s32[384]{0:T(512)S(1)} %get-tuple-element.33), kind=kOutput, calls=%fused_computation.8 | convolution fusion | flops 907640832 | bytes 2362368 | tf_op jit(solution)/shard_map/dot_general | solution.py:52
  139.0 3.9 %all-to-all-start.4 = ((bf16[16,72,512]{2,1,0:T(8,128)(2,1)}), bf16[16,72,512]{2,1,0:T(8,128)(2,1)S(1)}, u32[]{:S(2)}, u32[]{:S(2)}) async-start(bf16[16,72,512]{2,1,0:T(8,128)(2,1)} %bitcast.12), calls=%async_computation.4 | async-start | bytes 2359296 | tf_op jit(solution)/shard_map/all_to_all | solution.py:54
  142.9 3.1 %dynamic-slice_bitcast_fusion = bf16[512,2048]{1,0:T(8,128)(2,1)} fusion(bf16[1,4,512,2048]{3,2,1,0:T(8,128)(2,1)} %get-tuple-element.12, s32[]{:T(128)S(6)} %select_n.96), kind=kLoop, calls=%fused_computation.12 | loop fusion | bytes 4194308 | tf_op jit(solution)/shard_map/jit(dynamic_index_in_dim)/squeeze | solution.py:56
  146.2 30.5 %all-gather.5.cloned.1.call-done = bf16[8,4,64,512]{3,2,1,0:T(8,128)(2,1)} async-done(((bf16[4,4,64,512]{3,2,1,0:T(8,128)(2,1)}), bf16[8,4,64,512]{3,2,1,0:T(8,128)(2,1)}) %all-gather.5.cloned.1.call-update) | async-done | bytes 2097168 | tf_op jit(solution)/shard_map/all_gather | solution.py:32
  176.6 2.5 %fusion.58 = (bf16[1,8,64,512]{3,2,0,1:T(8,128)(2,1)}, bf16[1,8,64,512]{3,2,0,1:T(8,128)(2,1)S(1)}, bf16[1,8,64,512]{3,2,0,1:T(8,128)(2,1)S(1)}, bf16[1,8,64,512]{3,2,0,1:T(8,128)(2,1)S(1)}) fusion(bf16[4,8,64,512]{3,2,0,1:T(8,128)(2,1)} %bitcast.67), kind=kLoop, calls=%fused_computation.119 | loop fusion | bytes 4194304 | tf_op jit(solution)/shard_map/slice | solution.py:62
  181.0 2.4 %fusion.37 = f32[1152,512]{1,0:T(8,128)S(1)} fusion(bf16[1152,512]{1,0:T(8,128)(2,1)S(1)} %bitcast.62, bf16[512,2048]{1,0:T(8,128)(2,1)} %dynamic-slice_bitcast_fusion), kind=kOutput, calls=%fused_computation.59 | convolution fusion | flops 603979776 | bytes 4063232 | tf_op jit(solution)/shard_map/dot_general | solution.py:61
  190.4 3.8 %all-to-all-start.6 = ((bf16[16,8,72]{2,1,0:T(8,128)(2,1)}), bf16[16,8,72]{2,1,0:T(8,128)(2,1)S(1)}, u32[]{:S(2)}, u32[]{:S(2)}) async-start(bf16[16,8,72]{2,1,0:T(8,128)(2,1)} %copy.43), calls=%async_computation.6 | async-start | bytes 65536 | tf_op jit(solution)/shard_map/all_to_all | solution.py:81
  194.1 5.2 %multiply_convert_fusion = bf16[1152,512]{1,0:T(8,128)(2,1)} fusion(f32[1152,512]{1,0:T(8,128)} %copy-done.6, f32[1152,512]{1,0:T(8,128)} %copy-done.5, f32[1152,512]{1,0:T(8,128)} %copy-done.4, f32[1152,512]{1,0:T(8,128)S(1)} %copy-done.3, f32[1152]{0:T(1024)S(1)} %get-tuple-element.8, pred[1152]{0:T(1024)(128)(4,1)S(1)} %get-tuple-element.25, ...), kind=kLoop, calls=%fused_computation.10 | loop fusion | flops 3538944 | bytes 10626048 | tf_op jit(solution)/shard_map/convert_element_type | solution.py:73
  199.7 4.7 %all-to-all-start.7 = ((bf16[16,72,512]{2,1,0:T(8,128)(2,1)}), bf16[16,72,512]{2,1,0:T(8,128)(2,1)S(1)}, u32[]{:S(2)}, u32[]{:S(2)}) async-start(bf16[16,72,512]{2,1,0:T(8,128)(2,1)} %bitcast.65), calls=%async_computation.7 | async-start | bytes 2359296 | tf_op jit(solution)/shard_map/all_to_all | solution.py:74
  206.0 16.0 %all-to-all-done.7 = bf16[16,72,512]{2,1,0:T(8,128)(2,1)S(1)} async-done(((bf16[16,72,512]{2,1,0:T(8,128)(2,1)}), bf16[16,72,512]{2,1,0:T(8,128)(2,1)S(1)}, u32[]{:S(2)}, u32[]{:S(2)}) %all-to-all-start.7) | async-done | bytes 1179680 | tf_op jit(solution)/shard_map/all_to_all | solution.py:74
  (108 shorter events, 34.4 us)
Async XLA Ops:
  7.2 18.6 %copy-start = (bf16[384,512]{1,0:T(8,128)(2,1)S(1)}, bf16[384,512]{1,0:T(8,128)(2,1)}, u32[]{:S(2)}) copy-start(bf16[384,512]{1,0:T(8,128)(2,1)} %param.5) | copy-start | bytes 1179652
  10.5 11.7 %all-to-all-start = ((bf16[16,2,72]{2,1,0:T(2,128)(2,1)}), bf16[16,2,72]{2,1,0:T(2,128)(2,1)S(1)}, u32[]{:S(2)}, u32[]{:S(2)}) async-start(bf16[16,2,72]{2,1,0:T(2,128)(2,1)} %copy.34), calls=%async_computation | async-start | bytes 16384 | tf_op jit(solution)/shard_map/all_to_all | solution.py:45
  22.2 17.4 %all-to-all-start.2 = ((bf16[4,4,64,512]{3,2,1,0:T(8,128)(2,1)}), bf16[4,4,64,512]{3,2,1,0:T(8,128)(2,1)S(1)}, u32[]{:S(2)}, u32[]{:S(2)}) async-start(bf16[4,4,64,512]{3,2,1,0:T(8,128)(2,1)} %get-tuple-element.19), calls=%async_computation.2 | async-start | bytes 2097152 | tf_op jit(solution)/shard_map/all_to_all | solution.py:31
  39.6 3.8 %copy-start.14 = (bf16[4,4,64,512]{3,2,1,0:T(8,128)(2,1)}, bf16[4,4,64,512]{3,2,1,0:T(8,128)(2,1)S(1)}, u32[]{:S(2)}) copy-start(bf16[4,4,64,512]{3,2,1,0:T(8,128)(2,1)S(1)} %all-to-all-done.2) | copy-start | bytes 3145732
  39.6 21.8 %all-to-all-start.1 = ((bf16[16,72,512]{2,1,0:T(8,128)(2,1)}), bf16[16,72,512]{2,1,0:T(8,128)(2,1)S(1)}, u32[]{:S(2)}, u32[]{:S(2)}) async-start(bf16[16,72,512]{2,1,0:T(8,128)(2,1)} %bitcast.68), calls=%async_computation.1 | async-start | bytes 2359296 | tf_op jit(solution)/shard_map/all_to_all | solution.py:54
  43.3 60.4 %all-gather.3.cloned.1.call-start = ((), (), s32[]{:S(2)}) async-start(), calls=%async_computation.8 | async-start | bytes 3145728 | tf_op jit(solution)/shard_map/all_gather | solution.py:32
  61.5 52.1 %all-to-all-start.5 = ((bf16[4,4,64,512]{3,2,1,0:T(8,128)(2,1)}), bf16[4,4,64,512]{3,2,1,0:T(8,128)(2,1)S(1)}, u32[]{:S(2)}, u32[]{:S(2)}) async-start(bf16[4,4,64,512]{3,2,1,0:T(8,128)(2,1)} %get-tuple-element.18), calls=%async_computation.5 | async-start | bytes 2097152 | tf_op jit(solution)/shard_map/all_to_all | solution.py:31
  65.0 3.5 %copy-start.12 = (bf16[512,2048]{1,0:T(8,128)(2,1)S(1)}, bf16[512,2048]{1,0:T(8,128)(2,1)}, u32[]{:S(2)}) copy-start(bf16[512,2048]{1,0:T(8,128)(2,1)} %dynamic-slice_bitcast_fusion.1) | copy-start | bytes 6291460
  103.8 2.3 copy-start.7
  105.6 1.8 copy-start.8
  108.3 1.8 copy-start.10
  113.6 3.8 %copy-start.13 = (bf16[4,4,64,512]{3,2,1,0:T(8,128)(2,1)}, bf16[4,4,64,512]{3,2,1,0:T(8,128)(2,1)S(1)}, u32[]{:S(2)}) copy-start(bf16[4,4,64,512]{3,2,1,0:T(8,128)(2,1)S(1)} %all-to-all-done.5) | copy-start | bytes 3145732
  113.6 22.9 %all-to-all-start.3 = ((bf16[16,72,512]{2,1,0:T(8,128)(2,1)}), bf16[16,72,512]{2,1,0:T(8,128)(2,1)S(1)}, u32[]{:S(2)}, u32[]{:S(2)}) async-start(bf16[16,72,512]{2,1,0:T(8,128)(2,1)} %bitcast.10), calls=%async_computation.3 | async-start | bytes 2359296 | tf_op jit(solution)/shard_map/all_to_all | solution.py:74
  117.3 59.3 %all-gather.5.cloned.1.call-start = ((), (), s32[]{:S(2)}) async-start(), calls=%async_computation.9 | async-start | bytes 3145728 | tf_op jit(solution)/shard_map/all_gather | solution.py:32
  139.0 40.2 %all-to-all-start.4 = ((bf16[16,72,512]{2,1,0:T(8,128)(2,1)}), bf16[16,72,512]{2,1,0:T(8,128)(2,1)S(1)}, u32[]{:S(2)}, u32[]{:S(2)}) async-start(bf16[16,72,512]{2,1,0:T(8,128)(2,1)} %bitcast.12), calls=%async_computation.4 | async-start | bytes 2359296 | tf_op jit(solution)/shard_map/all_to_all | solution.py:54
  181.0 4.2 %copy-start.2 = (f32[1152,512]{1,0:T(8,128)}, f32[1152,512]{1,0:T(8,128)S(1)}, u32[]{:S(2)}) copy-start(f32[1152,512]{1,0:T(8,128)S(1)} %fusion.39) | copy-start | bytes 7077892
  181.0 2.6 %copy-start.11 = (bf16[512,2048]{1,0:T(8,128)(2,1)S(1)}, bf16[512,2048]{1,0:T(8,128)(2,1)}, u32[]{:S(2)}) copy-start(bf16[512,2048]{1,0:T(8,128)(2,1)} %dynamic-slice_bitcast_fusion) | copy-start | bytes 6291460
  183.6 3.1 %copy-start.4 = (f32[1152,512]{1,0:T(8,128)}, f32[1152,512]{1,0:T(8,128)S(1)}, u32[]{:S(2)}) copy-start(f32[1152,512]{1,0:T(8,128)S(1)} %fusion.37) | copy-start | bytes 7077892
  184.4 3.2 %copy-start.5 = (f32[1152,512]{1,0:T(8,128)}, f32[1152,512]{1,0:T(8,128)S(1)}, u32[]{:S(2)}) copy-start(f32[1152,512]{1,0:T(8,128)S(1)} %fusion.35) | copy-start | bytes 7077892
  185.2 3.3 %copy-start.6 = (f32[1152,512]{1,0:T(8,128)}, f32[1152,512]{1,0:T(8,128)S(1)}, u32[]{:S(2)}) copy-start(f32[1152,512]{1,0:T(8,128)S(1)} %fusion.33) | copy-start | bytes 7077892
  188.5 5.6 %copy-start.3 = (f32[1152,512]{1,0:T(8,128)S(1)}, f32[1152,512]{1,0:T(8,128)}, u32[]{:S(2)}) copy-start(f32[1152,512]{1,0:T(8,128)} %copy-done.2) | copy-start | bytes 7077892
  190.4 9.3 %all-to-all-start.6 = ((bf16[16,8,72]{2,1,0:T(8,128)(2,1)}), bf16[16,8,72]{2,1,0:T(8,128)(2,1)S(1)}, u32[]{:S(2)}, u32[]{:S(2)}) async-start(bf16[16,8,72]{2,1,0:T(8,128)(2,1)} %copy.43), calls=%async_computation.6 | async-start | bytes 65536 | tf_op jit(solution)/shard_map/all_to_all | solution.py:81
  199.7 22.3 %all-to-all-start.7 = ((bf16[16,72,512]{2,1,0:T(8,128)(2,1)}), bf16[16,72,512]{2,1,0:T(8,128)(2,1)S(1)}, u32[]{:S(2)}, u32[]{:S(2)}) async-start(bf16[16,72,512]{2,1,0:T(8,128)(2,1)} %bitcast.65), calls=%async_computation.7 | async-start | bytes 2359296 | tf_op jit(solution)/shard_map/all_to_all | solution.py:74
  204.4 19.0 %copy-start.1 = (bf16[384,512]{1,0:T(8,128)(2,1)S(1)}, bf16[384,512]{1,0:T(8,128)(2,1)}, u32[]{:S(2)}) copy-start(bf16[384,512]{1,0:T(8,128)(2,1)} %param.5) | copy-start | bytes 1179652
  (2 other events, 3.2 us)
Sparse Core Ops, SparseCore 0:
  45.7 58.0 all-gather.2
  119.7 56.8 all-gather.4

commit v2 on v1

v2 whole, which is shorter than its diff:
```python
import functools

import jax
import jax.numpy as jnp
from jax import lax
from jax.experimental import pallas as pl
from jax.experimental.pallas import tpu as pltpu
from jax.sharding import Mesh, PartitionSpec as P

OUTCOMES = 4
ORBITALS = 2
LANES = 128
CHUNKS = 4
MESH = pl.DeviceIdType.MESH
F32 = jnp.float32
BF16 = jnp.bfloat16


def kernel(
    sizes,
    vec_ref, sec_ref, out_ref, sec_t_ref, site_ref, env_ref,
    prob_ref, fin_ref,
    fs0, fr0, fs1, fr1, rs0, rr0, rs1, rr1,
    site_v, env_in, env_w, hot_t, kept,
    site_sem, fsend, frecv, rsend, rrecv, esend, erecv,
):
    n_sec, n_grp, n_own, cap = sizes
    n = n_sec * n_own
    n_row = n_grp * n_own
    samples, width = vec_ref.shape
    depth = env_ref.shape[3]
    blocks = width // LANES
    per_block = LANES // depth
    per_chunk = n // CHUNKS
    rows = per_chunk * cap
    fs, fr, rs, rr = (fs0, fs1), (fr0, fr1), (rs0, rs1), (rr0, rr1)

    si, gi, oi = lax.axis_index("sector"), lax.axis_index("grp"), lax.axis_index("own")
    me = si * n_own + oi
    row_me = gi * n_own + oi

    def peer(pos):
        pos = lax.rem(pos, n)
        return (lax.div(pos, n_own), gi, lax.rem(pos, n_own))

    def row_peer(pos):
        pos = lax.rem(pos, n_row)
        return (si, lax.div(pos, n_own), lax.rem(pos, n_own))

    def loop(low, high, body):
        lax.fori_loop(low, high, lambda i, c: (body(i), c)[1], 0)

    site_copies = [
        pltpu.make_async_copy(site_ref.at[k, oi], site_v.at[k], site_sem.at[k]) for k in range(ORBITALS)
    ]
    for copy in site_copies:
        copy.start()

    barrier = pltpu.get_barrier_semaphore()

    def greet(r):
        pl.semaphore_signal(barrier, inc=1, device_id=peer(me + r), device_id_type=MESH)

    def greet_far(j):
        pl.semaphore_signal(
            barrier,
            inc=1,
            device_id=(si, lax.rem(gi + 1 + lax.div(j, n_own), n_grp), lax.rem(j, n_own)),
            device_id_type=MESH,
        )

    loop(1, n, greet)
    loop(0, (n_grp - 1) * n_own, greet_far)

    def env_part(k, origin, t):
        column = lax.rem(lax.div(origin, per_block) + t, blocks) * LANES
        return env_in.at[
            k, :, pl.ds(pl.multiple_of(origin * depth, depth), depth), pl.ds(pl.multiple_of(column, LANES), LANES)
        ]

    def has_third(origin):
        m = lax.div(origin, per_block)
        return jnp.logical_or(m == 0, m == blocks - 1)

    def env_copy(k, d, t):
        target = row_peer(row_me + d)
        column = lax.rem(lax.div(row_me, per_block) + t, blocks) * LANES
        return pltpu.make_async_remote_copy(
            src_ref=env_ref.at[k, target[2], :, :, pl.ds(pl.multiple_of(column, LANES), LANES)],
            dst_ref=env_part(k, row_me, t),
            send_sem=esend.at[k, d, t],
            recv_sem=erecv.at[k, d, t],
            device_id=target,
            device_id_type=MESH,
        )

    def env_own(k, t):
        column = lax.rem(lax.div(row_me, per_block) + t, blocks) * LANES
        return pltpu.make_async_copy(
            env_ref.at[k, oi, :, :, pl.ds(pl.multiple_of(column, LANES), LANES)],
            env_part(k, row_me, t),
            erecv.at[k, 0, t],
        )

    def env_arrival(k, d, t):
        origin = lax.rem(row_me - d + n_row, n_row)
        part = env_part(k, origin, t)
        return pltpu.make_async_remote_copy(
            src_ref=part,
            dst_ref=part,
            send_sem=esend.at[k, d, t],
            recv_sem=erecv.at[k, d, t],
            device_id=row_peer(row_me + d),
            device_id_type=MESH,
        )

    def env_start(k):
        def one(d):
            env_copy(k, d, 0).start()
            env_copy(k, d, 1).start()

            @pl.when(has_third(row_me))
            def _():
                env_copy(k, d, 2).start()

        env_own(k, 0).start()
        env_own(k, 1).start()

        @pl.when(has_third(row_me))
        def _():
            env_own(k, 2).start()

        loop(1, n_row, one)

    def env_wait(k):
        def one(d):
            env_arrival(k, d, 0).wait_recv()
            env_arrival(k, d, 1).wait_recv()

            @pl.when(has_third(lax.rem(row_me - d + n_row, n_row)))
            def _():
                env_arrival(k, d, 2).wait_recv()

        env_own(k, 0).wait()
        env_own(k, 1).wait()

        @pl.when(has_third(row_me))
        def _():
            env_own(k, 2).wait()

        loop(1, n_row, one)

    def env_sent(k):
        def one(d):
            env_copy(k, d, 0).wait_send()
            env_copy(k, d, 1).wait_send()

            @pl.when(has_third(row_me))
            def _():
                env_copy(k, d, 2).wait_send()

        loop(1, n_row, one)

    def env_build(k):
        for m in range(blocks):
            for t in range(3 if m in (0, blocks - 1) else 2):
                c = (m + t) % blocks
                at = (slice(m * LANES, (m + 1) * LANES), slice(c * LANES, (c + 1) * LANES))
                part = env_in[k, :, at[0], at[1]]
                env_w[:, at[0], at[1]] = part if t == 0 else part + part

    def relative(labels):
        shifted = labels - me
        return jnp.where(shifted < 0, shifted + n, shifted).astype(F32)

    first = lax.broadcasted_iota(jnp.int32, (samples, samples), 0)
    second = lax.broadcasted_iota(jnp.int32, (samples, samples), 1)
    upper = (first < second).astype(F32).astype(BF16)
    lower = (first > second).astype(F32).astype(BF16)
    slot_rows = []
    marks = []
    lane = lax.broadcasted_iota(jnp.int32, (samples, LANES), 1)
    slot_lane = lax.broadcasted_iota(jnp.int32, (samples, n * cap), 1).astype(F32)
    for k in range(ORBITALS):
        label = relative(sec_t_ref[k : k + 1, :])
        hot = (lax.broadcasted_iota(jnp.int32, (n, samples), 0).astype(F32) == label).astype(F32)
        before = jnp.dot(hot.astype(BF16), upper, preferred_element_type=F32)
        slot_rows.append(label * cap + jnp.sum(before * hot, axis=0, keepdims=True))
        label = relative(sec_ref[:, k : k + 1])
        hot = (lane.astype(F32) == label).astype(F32)
        before = jnp.dot(lower, hot.astype(BF16), preferred_element_type=F32)
        slot = label * cap + jnp.sum(before * hot, axis=1, keepdims=True)
        hot_t[k] = (slot_lane == slot).astype(F32).astype(BF16)
        marks.append((lane == out_ref[:, k : k + 1] + OUTCOMES * k).astype(F32).astype(BF16))

    env_w[...] = jnp.zeros_like(env_w)

    pl.semaphore_wait(barrier, n - 1 + (n_grp - 1) * n_own)

    def piece(ref, r):
        return ref.at[pl.ds(pl.multiple_of(r * cap, 16), cap)]

    def out_copy(k, r):
        return pltpu.make_async_remote_copy(
            src_ref=piece(fs[k], r),
            dst_ref=piece(fr[k], r),
            send_sem=fsend.at[k, r],
            recv_sem=frecv.at[k, r],
            device_id=peer(me + r),
            device_id_type=MESH,
        )

    def back_copy(k, r):
        return pltpu.make_async_remote_copy(
            src_ref=piece(rs[k], r),
            dst_ref=piece(rr[k], r),
            send_sem=rsend.at[k, r],
            recv_sem=rrecv.at[k, r],
            device_id=peer(me - r + n),
            device_id_type=MESH,
        )

    def in_chunk(c, act):
        def one(r):
            @pl.when(r > 0)
            def _():
                act(r)

        loop(c * per_chunk, (c + 1) * per_chunk, one)

    def span(c):
        return pl.ds(pl.multiple_of(c * rows, 16), rows)

    current = vec_ref[...]
    for k in range(ORBITALS):

        def pack(c, k=k, current=current):
            place = (lax.broadcasted_iota(jnp.int32, (rows, samples), 0) + c * rows).astype(F32)
            hot = (place == slot_rows[k]).astype(F32).astype(BF16)
            packed = jnp.dot(hot, current, preferred_element_type=F32).astype(BF16)
            fs[k][span(c), :width] = packed
            if k == 0:
                other = (place == slot_rows[1]).astype(F32).astype(BF16)
                mark = jnp.dot(hot, marks[0], preferred_element_type=F32)
                mark = mark + jnp.dot(other, marks[1], preferred_element_type=F32)
                fs[0][span(c), width:] = mark.astype(BF16)
            in_chunk(c, lambda r: out_copy(k, r).start())

        loop(0, CHUNKS, pack)
        fr[k][:cap] = fs[k][:cap]
        if k == 0:
            env_start(0)
        site_copies[k].wait()
        env_wait(k)
        env_build(k)
        if k == 0:
            env_start(1)

        def work(c, k=k):
            in_chunk(c, lambda r: out_copy(k, r).wait_recv())
            left = fr[k][span(c), :width]
            mark = fr[0][span(c), width:].astype(F32)
            weights = []
            chosen = []
            picked = jnp.zeros((rows, width), F32)
            for s in range(OUTCOMES):
                amp = jnp.dot(left, site_v[k, :, s * width : (s + 1) * width], preferred_element_type=F32)
                image = jnp.dot(amp.astype(BF16), env_w[s], preferred_element_type=F32)
                weights.append(jnp.sum(image * amp, axis=1, keepdims=True))
                at = OUTCOMES * k + s
                chosen.append(mark[:, at : at + 1])
                picked = jnp.where(chosen[s] > 0.0, amp, picked)
            total = weights[0] + weights[1] + weights[2] + weights[3]
            filled = (chosen[0] + chosen[1] + chosen[2] + chosen[3]) > 0.0
            weight = jnp.zeros_like(total)
            for s in range(OUTCOMES):
                weight = jnp.where(chosen[s] > 0.0, weights[s], weight)
            total = jnp.where(filled, total, 1.0)
            scale = lax.rsqrt(jnp.where(filled, weight, 1.0) / width)
            rs[k][span(c), :width] = (picked * scale).astype(BF16)
            lanes = lax.broadcasted_iota(jnp.int32, (rows, LANES), 1)
            probs = jnp.zeros((rows, LANES), F32) if k == 0 else kept[span(c), :].astype(F32)
            for s in range(OUTCOMES):
                value = jnp.where(filled, weights[s] / total, 0.0)
                probs = jnp.where(lanes == OUTCOMES * k + s, value, probs)
            if k == 0:
                kept[span(c), :] = probs.astype(BF16)
            else:
                rs[1][span(c), width:] = probs.astype(BF16)
            in_chunk(c, lambda r: back_copy(k, r).start())

        loop(0, CHUNKS, work)
        rr[k][:cap] = rs[k][:cap]
        loop(1, n, lambda r, k=k: back_copy(k, r).wait_recv())
        current = jnp.dot(hot_t[k], rr[k][:, :width], preferred_element_type=F32).astype(BF16)
    fin_ref[...] = current
    tail = rr[1][:, width:]
    low = jnp.dot(hot_t[0], tail, preferred_element_type=F32)
    high = jnp.dot(hot_t[1], tail, preferred_element_type=F32)
    prob_ref[...] = jnp.where(lane < OUTCOMES, low, high)[:, : OUTCOMES * ORBITALS].astype(BF16)

    for k in range(ORBITALS):
        loop(1, n, lambda r, k=k: out_copy(k, r).wait_send())
        loop(1, n, lambda r, k=k: back_copy(k, r).wait_send())
        env_sent(k)


def local(sizes, vectors, sectors, outcomes, sites, environments):
    n_sec, n_grp, n_own, cap = sizes
    n, n_row = n_sec * n_own, n_grp * n_own
    samples, width = vectors.shape
    slots = n * cap
    vmem = pl.BlockSpec(memory_space=pltpu.VMEM)
    hbm = pl.BlockSpec(memory_space=pl.ANY)
    dma = pltpu.SemaphoreType.DMA
    wide, plain = pltpu.VMEM((slots, width + LANES), BF16), pltpu.VMEM((slots, width), BF16)
    return pl.pallas_call(
        functools.partial(kernel, sizes),
        out_shape=(
            jax.ShapeDtypeStruct((samples, ORBITALS * OUTCOMES), BF16),
            jax.ShapeDtypeStruct((samples, width), BF16),
        ),
        in_specs=[vmem, vmem, vmem, vmem, hbm, hbm],
        out_specs=(vmem, vmem),
        scratch_shapes=[
            wide, wide, plain, plain, plain, plain, wide, wide,
            pltpu.VMEM((ORBITALS, width, OUTCOMES * width), BF16),
            pltpu.VMEM((ORBITALS, OUTCOMES, width, width), BF16),
            pltpu.VMEM((OUTCOMES, width, width), BF16),
            pltpu.VMEM((ORBITALS, samples, slots), BF16),
            pltpu.VMEM((slots, LANES), BF16),
            dma((ORBITALS,)),
            dma((ORBITALS, n)), dma((ORBITALS, n)), dma((ORBITALS, n)), dma((ORBITALS, n)),
            dma((ORBITALS, n_row, 3)), dma((ORBITALS, n_row, 3)),
        ],
        compiler_params=pltpu.CompilerParams(
            collective_id=0, has_side_effects=True, vmem_limit_bytes=56 * 1024 * 1024
        ),
    )(vectors, sectors, outcomes, sectors.T, sites, environments)


def solution(mesh):
    def run(vectors, sectors, outcomes, sites, environments):
        sector_size, section_size = mesh.devices.shape
        owners = sites.shape[1] // sector_size
        split = Mesh(
            mesh.devices.reshape(sector_size, section_size // owners, owners), ("sector", "grp", "own")
        )
        every = P(("sector", "grp", "own"), None)
        per_device = vectors.shape[0] // mesh.devices.size
        cap = -(-3 * per_device // sites.shape[1])
        cap = -(-cap // 16) * 16
        return jax.shard_map(
            functools.partial(local, (sector_size, section_size // owners, owners, cap)),
            mesh=split,
            in_specs=(
                every,
                every,
                every,
                P(None, "sector", None, None),
                P(None, "sector", None, ("grp", "own"), None),
            ),
            out_specs=(every, every),
            check_vma=False,
        )(vectors, sectors, outcomes, sites, environments)

    return run
```

time: 232 us -> 141 us (0.61)
  Pallas kernels: 0 us -> 133 us
  waiting for transfers between devices: 112 us -> 0 us
  starting transfers between devices: 33.2 us -> 0 us
  matrix products: 29.7 us -> 0 us
  local copies, waits for them, and re-layouts: 31.4 us -> 6.33 us
  between operations: 14.6 us -> 0.64 us
  other arithmetic: 9.91 us -> 0 us
    pallas_call x0 -> x1, Pallas kernels: none -> 133 us  [local(): pl.pallas_call(functools.partial(kernel, sizes), out_shape=(jax.ShapeDtyp...]
    all_gather x2 -> x0, waiting for transfers between devices: 59.3 us -> none  [local(): whole = lax.all_gather(part, 'grp', axis=0, tiled=True)]
    all_to_all x8 -> x0, waiting for transfers between devices: 50.9 us -> none  [the longest x2 34.4 us: local(): lax.all_to_all(advanced.reshape(sector_total, capacity, width), peers, sp...]
    all_to_all x8 -> x0, starting transfers between devices: 33.1 us -> none  [the longest x2 8.5 us: local(): lax.all_to_all(advanced.reshape(sector_total, capacity, width), peers, sp...]
    dot_general x23 -> x0, matrix products: 29.7 us -> none  [the longest x8 15.7 us: local(): jnp.dot(rows_in, site[:, s * width:(s + 1) * width], preferred_element_ty...]
    slice x5 -> x0, local copies, waits for them, and re-layouts: 17.2 us -> none  [the longest x1 12 us: local(): site = lax.dynamic_index_in_dim(sites[k], own, 0, keepdims=False)]
    squeeze x3 -> x0, local copies, waits for them, and re-layouts: 9.63 us -> none  [the longest x2 6.5 us: local(): site = lax.dynamic_index_in_dim(sites[k], own, 0, keepdims=False)]
    convert_element_type x4 -> x0, other arithmetic: 7.74 us -> none  [the longest x2 7.72 us: local(): advanced = (picked * scale[:, None]).astype(jnp.bfloat16)]
  transfers between devices with their start and end apart: 10 -> 0, of which waited for: 8 -> 0; matrix products, arithmetic and copies ran while one was open for 23% -> 0% of each run, Pallas kernels for 0% -> 0%
where the time goes in v2:
time: 141 us; the launch traced here: 140 us
  Pallas kernels  133 us (94%)
  local copies, waits for them, and re-layouts  6.33 us (4%)
    pallas_call x1, Pallas kernels, local(): pl.pallas_call(functools.partial(kernel, sizes), out_shape=(jax.ShapeDtyp...  133 us
    unnamed x3, local copies, waits for them, and re-layouts  4.78 us

profile of v2, /device:TPU:0, one launch (start us, length us, event | category | flops | bytes accessed | tf_op | source)
XLA Modules:
  0.0 139.9 jit_solution(9108193397381591302)
XLA Ops:
  0.6 1.5 %copy.8.out_ref = s32[384,2]{1,0:T(8,128)} copy(s32[384,2]{0,1:T(2,128)} %param.7) | data formatting | bytes 6144 | tf_op args[2]
  2.1 1.5 %copy.7.sec_ref = s32[384,2]{1,0:T(8,128)} copy(s32[384,2]{0,1:T(2,128)} %param.6) | data formatting | bytes 6144 | tf_op args[1]
  3.6 132.9 %shard_map.68 = (bf16[384,8]{1,0:T(8,128)(2,1)}, bf16[384,512]{1,0:T(8,128)(2,1)}) custom-call(bf16[384,512]{1,0:T(8,128)(2,1)} %vec_ref.1, s32[384,2]{1,0:T(8,128)} %copy.7.sec_ref, s32[384,2]{1,0:T(8,128)} %copy.8.out_ref, s32[2,384]{1,0:T(2,128)} %bitcast.1, bf16[2,4,512,2048]{3,2,1,0:T(8,128)(2,1)} %site_ref.1, bf16[2,4,4,64,512]{4,3,2,1,0:T(8,128)(2,1)} %env_ref.1), custom_call_target="tpu_custom_call" | custom-call | tf_op jit(solution)/shard_map/pallas_call | solution.py:317
  136.5 1.6 %copy.9 = bf16[384,8]{0,1:T(8,128)(2,1)} copy(bf16[384,8]{1,0:T(8,128)(2,1)} %get-tuple-element.2) | data formatting | bytes 12288 | tf_op jit(solution)/shard_map/pallas_call | solution.py:317
  138.1 1.8 %copy.11 = bf16[384,512]{1,0:T(8,128)(2,1)} copy(bf16[384,512]{1,0:T(8,128)(2,1)} %get-tuple-element.7) | data formatting | bytes 786432

commit v3 on v2

--- a/solution.py
+++ b/solution.py
@@ -11,6 +11,7 @@
 ORBITALS = 2
 LANES = 128
 CHUNKS = 4
+MARKS = 16
 MESH = pl.DeviceIdType.MESH
 F32 = jnp.float32
 BF16 = jnp.bfloat16
@@ -18,11 +19,12 @@
 
 def kernel(
     sizes,
-    vec_ref, sec_ref, out_ref, sec_t_ref, site_ref, env_ref,
+    vec_ref, sec_ref, out_ref, site_ref, env_ref,
     prob_ref, fin_ref,
     fs0, fr0, fs1, fr1, rs0, rr0, rs1, rr1,
-    site_v, env_in, env_w, hot_t, kept,
-    site_sem, fsend, frecv, rsend, rrecv, esend, erecv,
+    mark_s, mark_r, prob_s, prob_r,
+    site_v, env_in, env_w, amps, hot_t,
+    site_sem, fsend, frecv, rsend, rrecv, esend, erecv, msend, mrecv, psend, precv,
 ):
     n_sec, n_grp, n_own, cap = sizes
     n = n_sec * n_own
@@ -176,29 +178,63 @@
     first = lax.broadcasted_iota(jnp.int32, (samples, samples), 0)
     second = lax.broadcasted_iota(jnp.int32, (samples, samples), 1)
     upper = (first < second).astype(F32).astype(BF16)
-    lower = (first > second).astype(F32).astype(BF16)
     slot_rows = []
-    marks = []
-    lane = lax.broadcasted_iota(jnp.int32, (samples, LANES), 1)
-    slot_lane = lax.broadcasted_iota(jnp.int32, (samples, n * cap), 1).astype(F32)
+    slot_columns = []
+    marks = jnp.zeros((MARKS, n * LANES), F32)
+    mark_row = lax.broadcasted_iota(jnp.int32, (MARKS, samples), 0)
+    slot_lane = lax.broadcasted_iota(jnp.int32, (samples, n * LANES), 1).astype(F32)
     for k in range(ORBITALS):
-        label = relative(sec_t_ref[k : k + 1, :])
+        label = relative(sec_ref[k : k + 1, :])
         hot = (lax.broadcasted_iota(jnp.int32, (n, samples), 0).astype(F32) == label).astype(F32)
         before = jnp.dot(hot.astype(BF16), upper, preferred_element_type=F32)
-        slot_rows.append(label * cap + jnp.sum(before * hot, axis=0, keepdims=True))
-        label = relative(sec_ref[:, k : k + 1])
-        hot = (lane.astype(F32) == label).astype(F32)
-        before = jnp.dot(lower, hot.astype(BF16), preferred_element_type=F32)
-        slot = label * cap + jnp.sum(before * hot, axis=1, keepdims=True)
-        hot_t[k] = (slot_lane == slot).astype(F32).astype(BF16)
-        marks.append((lane == out_ref[:, k : k + 1] + OUTCOMES * k).astype(F32).astype(BF16))
+        place = jnp.sum(before * hot, axis=0, keepdims=True)
+        both = [label * cap + place, label * LANES + place]
+        columns = [jnp.sum(jnp.where(first == second, row, 0.0), axis=1, keepdims=True) for row in both]
+        slot_rows.append(both[0])
+        slot_columns.append(columns[0])
+        hot_t[k] = (slot_lane == columns[1]).astype(F32).astype(BF16)
+        mark = (mark_row == out_ref[k : k + 1, :] + OUTCOMES * k).astype(F32).astype(BF16)
+        marks = marks + jnp.dot(mark, hot_t[k], preferred_element_type=F32)
+    mark_s[...] = marks.astype(BF16)
+
+    row_at = lax.broadcasted_iota(jnp.int32, (rows, per_chunk * LANES), 0)
+    lane_at = lax.broadcasted_iota(jnp.int32, (rows, per_chunk * LANES), 1)
+    spread = jnp.zeros((rows, per_chunk * LANES), F32)
+    for j in range(per_chunk):
+        here = jnp.logical_and(row_at >= j * cap, row_at < (j + 1) * cap)
+        same = jnp.logical_and(here, lane_at - j * LANES == row_at - j * cap)
+        spread = jnp.where(same, 1.0, spread)
+    spread = spread.astype(BF16)
 
     env_w[...] = jnp.zeros_like(env_w)
 
     pl.semaphore_wait(barrier, n - 1 + (n_grp - 1) * n_own)
 
     def piece(ref, r):
-        return ref.at[pl.ds(pl.multiple_of(r * cap, 16), cap)]
+        return ref.at[pl.ds(pl.multiple_of(r * 2 * cap, 16), 2 * cap)]
+
+    def tile(ref, r):
+        return ref.at[:, pl.ds(pl.multiple_of(r * LANES, LANES), LANES)]
+
+    def mark_copy(r):
+        return pltpu.make_async_remote_copy(
+            src_ref=tile(mark_s, r),
+            dst_ref=tile(mark_r, r),
+            send_sem=msend.at[r],
+            recv_sem=mrecv.at[r],
+            device_id=peer(me + r),
+            device_id_type=MESH,
+        )
+
+    def prob_copy(r):
+        return pltpu.make_async_remote_copy(
+            src_ref=tile(prob_s, r),
+            dst_ref=tile(prob_r, r),
+            send_sem=psend.at[r],
+            recv_sem=precv.at[r],
+            device_id=peer(me - r + n),
+            device_id_type=MESH,
+        )
 
     def out_copy(k, r):
         return pltpu.make_async_remote_copy(
@@ -229,7 +265,63 @@
         loop(c * per_chunk, (c + 1) * per_chunk, one)
 
     def span(c):
-        return pl.ds(pl.multiple_of(c * rows, 16), rows)
+        return pl.ds(pl.multiple_of(c * 2 * rows, 16), 2 * rows)
+
+    def tiles(c):
+        return pl.ds(pl.multiple_of(c * per_chunk * LANES, LANES), per_chunk * LANES)
+
+    def flat(c):
+        return pl.ds(pl.multiple_of(c * rows, 8), rows)
+
+    half = width // 2
+
+    def encode(x):
+        parts = [x[:, :half].reshape(per_chunk, 1, cap, half), x[:, half:].reshape(per_chunk, 1, cap, half)]
+        return jnp.concatenate(parts, axis=1).reshape(2 * rows, half).astype(BF16)
+
+    def decode(x):
+        x = x.astype(F32).reshape(per_chunk, 2, cap, half)
+        return jnp.concatenate([x[:, 0].reshape(rows, half), x[:, 1].reshape(rows, half)], axis=1).astype(BF16)
+
+    def first_product(k, c, s, left):
+        return jnp.dot(left, site_v[k, :, s * width : (s + 1) * width], preferred_element_type=F32)
+
+    def branch(k, c, amp_of):
+        mark = lax.dot_general(
+            spread, mark_r[:, tiles(c)], (((1,), (1,)), ((), ())), preferred_element_type=F32
+        )
+        weights = []
+        chosen = []
+        picked = jnp.zeros((rows, width), F32)
+        for s in range(OUTCOMES):
+            amp = amp_of(s)
+            image = jnp.dot(amp.astype(BF16), env_w[s], preferred_element_type=F32)
+            weights.append(jnp.sum(image * amp, axis=1, keepdims=True))
+            at = OUTCOMES * k + s
+            chosen.append(mark[:, at : at + 1])
+            picked = jnp.where(chosen[s] > 0.0, amp, picked)
+        total = weights[0] + weights[1] + weights[2] + weights[3]
+        filled = (chosen[0] + chosen[1] + chosen[2] + chosen[3]) > 0.0
+        weight = jnp.zeros_like(total)
+        for s in range(OUTCOMES):
+            weight = jnp.where(chosen[s] > 0.0, weights[s], weight)
+        total = jnp.where(filled, total, 1.0)
+        scale = lax.rsqrt(jnp.where(filled, weight, 1.0) / width)
+        rs[k][span(c), :] = encode(picked * scale)
+        in_chunk(c, lambda r: back_copy(k, r).start())
+        lanes = lax.broadcasted_iota(jnp.int32, (rows, MARKS), 1)
+        probs = jnp.zeros((rows, MARKS), F32)
+        for s in range(OUTCOMES):
+            value = jnp.where(filled, weights[s] / total, 0.0)
+            probs = jnp.where(lanes == OUTCOMES * k + s, value, probs)
+        probs = lax.dot_general(
+            probs.astype(BF16), spread, (((0,), (0,)), ((), ())), preferred_element_type=F32
+        )
+        if k == 0:
+            prob_s[:, tiles(c)] = probs.astype(BF16)
+        else:
+            prob_s[:, tiles(c)] = (prob_s[:, tiles(c)].astype(F32) + probs).astype(BF16)
+            in_chunk(c, lambda r: prob_copy(r).start())
 
     current = vec_ref[...]
     for k in range(ORBITALS):
@@ -237,72 +329,65 @@
         def pack(c, k=k, current=current):
             place = (lax.broadcasted_iota(jnp.int32, (rows, samples), 0) + c * rows).astype(F32)
             hot = (place == slot_rows[k]).astype(F32).astype(BF16)
-            packed = jnp.dot(hot, current, preferred_element_type=F32).astype(BF16)
-            fs[k][span(c), :width] = packed
-            if k == 0:
-                other = (place == slot_rows[1]).astype(F32).astype(BF16)
-                mark = jnp.dot(hot, marks[0], preferred_element_type=F32)
-                mark = mark + jnp.dot(other, marks[1], preferred_element_type=F32)
-                fs[0][span(c), width:] = mark.astype(BF16)
+            fs[k][span(c), :] = encode(jnp.dot(hot, current, preferred_element_type=F32))
             in_chunk(c, lambda r: out_copy(k, r).start())
 
         loop(0, CHUNKS, pack)
-        fr[k][:cap] = fs[k][:cap]
+        fr[k][: 2 * cap] = fs[k][: 2 * cap]
         if k == 0:
             env_start(0)
+            loop(1, n, lambda r: mark_copy(r).start())
+            mark_r[:, :LANES] = mark_s[:, :LANES]
         site_copies[k].wait()
+
+        def lead(c, k=k):
+            in_chunk(c, lambda r: out_copy(k, r).wait_recv())
+            left = decode(fr[k][span(c), :])
+            for s in range(OUTCOMES):
+                amps[flat(c), s * width : (s + 1) * width] = first_product(k, c, s, left)
+
+        def rest(c, k=k):
+            branch(k, c, lambda s: amps[flat(c), s * width : (s + 1) * width])
+
+        def work(c, k=k):
+            in_chunk(c, lambda r: out_copy(k, r).wait_recv())
+            left = decode(fr[k][span(c), :])
+            branch(k, c, lambda s: first_product(k, c, s, left))
+
+        if k == 0:
+            loop(0, CHUNKS, lead)
+            loop(1, n, lambda r: mark_copy(r).wait_recv())
         env_wait(k)
         env_build(k)
         if k == 0:
             env_start(1)
-
-        def work(c, k=k):
-            in_chunk(c, lambda r: out_copy(k, r).wait_recv())
-            left = fr[k][span(c), :width]
-            mark = fr[0][span(c), width:].astype(F32)
-            weights = []
-            chosen = []
-            picked = jnp.zeros((rows, width), F32)
-            for s in range(OUTCOMES):
-                amp = jnp.dot(left, site_v[k, :, s * width : (s + 1) * width], preferred_element_type=F32)
-                image = jnp.dot(amp.astype(BF16), env_w[s], preferred_element_type=F32)
-                weights.append(jnp.sum(image * amp, axis=1, keepdims=True))
-                at = OUTCOMES * k + s
-                chosen.append(mark[:, at : at + 1])
-                picked = jnp.where(chosen[s] > 0.0, amp, picked)
-            total = weights[0] + weights[1] + weights[2] + weights[3]
-            filled = (chosen[0] + chosen[1] + chosen[2] + chosen[3]) > 0.0
-            weight = jnp.zeros_like(total)
-            for s in range(OUTCOMES):
-                weight = jnp.where(chosen[s] > 0.0, weights[s], weight)
-            total = jnp.where(filled, total, 1.0)
-            scale = lax.rsqrt(jnp.where(filled, weight, 1.0) / width)
-            rs[k][span(c), :width] = (picked * scale).astype(BF16)
-            lanes = lax.broadcasted_iota(jnp.int32, (rows, LANES), 1)
-            probs = jnp.zeros((rows, LANES), F32) if k == 0 else kept[span(c), :].astype(F32)
-            for s in range(OUTCOMES):
-                value = jnp.where(filled, weights[s] / total, 0.0)
-                probs = jnp.where(lanes == OUTCOMES * k + s, value, probs)
-            if k == 0:
-                kept[span(c), :] = probs.astype(BF16)
-            else:
-                rs[1][span(c), width:] = probs.astype(BF16)
-            in_chunk(c, lambda r: back_copy(k, r).start())
-
-        loop(0, CHUNKS, work)
-        rr[k][:cap] = rs[k][:cap]
-        loop(1, n, lambda r, k=k: back_copy(k, r).wait_recv())
-        current = jnp.dot(hot_t[k], rr[k][:, :width], preferred_element_type=F32).astype(BF16)
+            loop(0, CHUNKS, rest)
+        else:
+            loop(0, CHUNKS, work)
+        rr[k][: 2 * cap] = rs[k][: 2 * cap]
+
+        def gather(c, total, k=k):
+            in_chunk(c, lambda r: back_copy(k, r).wait_recv())
+            place = (lax.broadcasted_iota(jnp.int32, (samples, rows), 1) + c * rows).astype(F32)
+            hot = (place == slot_columns[k]).astype(F32).astype(BF16)
+            return total + jnp.dot(hot, decode(rr[k][span(c), :]), preferred_element_type=F32)
+
+        current = lax.fori_loop(0, CHUNKS, gather, jnp.zeros((samples, width), F32)).astype(BF16)
     fin_ref[...] = current
-    tail = rr[1][:, width:]
-    low = jnp.dot(hot_t[0], tail, preferred_element_type=F32)
-    high = jnp.dot(hot_t[1], tail, preferred_element_type=F32)
-    prob_ref[...] = jnp.where(lane < OUTCOMES, low, high)[:, : OUTCOMES * ORBITALS].astype(BF16)
+    prob_r[:, :LANES] = prob_s[:, :LANES]
+    loop(1, n, lambda r: prob_copy(r).wait_recv())
+    tail = prob_r[...]
+    side = (((1,), (1,)), ((), ()))
+    low = lax.dot_general(tail, hot_t[0], side, preferred_element_type=F32)
+    high = lax.dot_general(tail, hot_t[1], side, preferred_element_type=F32)
+    prob_ref[...] = jnp.where(mark_row < OUTCOMES, low, high)[: OUTCOMES * ORBITALS].astype(BF16)
 
     for k in range(ORBITALS):
         loop(1, n, lambda r, k=k: out_copy(k, r).wait_send())
         loop(1, n, lambda r, k=k: back_copy(k, r).wait_send())
         env_sent(k)
+    loop(1, n, lambda r: mark_copy(r).wait_send())
+    loop(1, n, lambda r: prob_copy(r).wait_send())
 
 
 def local(sizes, vectors, sectors, outcomes, sites, environments):
@@ -313,30 +398,33 @@
     vmem = pl.BlockSpec(memory_space=pltpu.VMEM)
     hbm = pl.BlockSpec(memory_space=pl.ANY)
     dma = pltpu.SemaphoreType.DMA
-    wide, plain = pltpu.VMEM((slots, width + LANES), BF16), pltpu.VMEM((slots, width), BF16)
-    return pl.pallas_call(
+    halves, tile = pltpu.VMEM((2 * slots, width // 2), BF16), pltpu.VMEM((MARKS, n * LANES), BF16)
+    probs, final = pl.pallas_call(
         functools.partial(kernel, sizes),
         out_shape=(
-            jax.ShapeDtypeStruct((samples, ORBITALS * OUTCOMES), BF16),
+            jax.ShapeDtypeStruct((ORBITALS * OUTCOMES, samples), BF16),
             jax.ShapeDtypeStruct((samples, width), BF16),
         ),
-        in_specs=[vmem, vmem, vmem, vmem, hbm, hbm],
+        in_specs=[vmem, vmem, vmem, hbm, hbm],
         out_specs=(vmem, vmem),
         scratch_shapes=[
-            wide, wide, plain, plain, plain, plain, wide, wide,
+            halves, halves, halves, halves, halves, halves, halves, halves,
+            tile, tile, tile, tile,
             pltpu.VMEM((ORBITALS, width, OUTCOMES * width), BF16),
             pltpu.VMEM((ORBITALS, OUTCOMES, width, width), BF16),
             pltpu.VMEM((OUTCOMES, width, width), BF16),
-            pltpu.VMEM((ORBITALS, samples, slots), BF16),
-            pltpu.VMEM((slots, LANES), BF16),
+            pltpu.VMEM((slots, OUTCOMES * width), F32),
+            pltpu.VMEM((ORBITALS, samples, n * LANES), BF16),
             dma((ORBITALS,)),
             dma((ORBITALS, n)), dma((ORBITALS, n)), dma((ORBITALS, n)), dma((ORBITALS, n)),
             dma((ORBITALS, n_row, 3)), dma((ORBITALS, n_row, 3)),
+            dma((n,)), dma((n,)), dma((n,)), dma((n,)),
         ],
         compiler_params=pltpu.CompilerParams(
             collective_id=0, has_side_effects=True, vmem_limit_bytes=56 * 1024 * 1024
         ),
-    )(vectors, sectors, outcomes, sectors.T, sites, environments)
+    )(vectors, sectors.T, outcomes.T, sites, environments)
+    return probs.T, final
 
 
 def solution(mesh):
@@ -349,7 +437,7 @@
         every = P(("sector", "grp", "own"), None)
         per_device = vectors.shape[0] // mesh.devices.size
         cap = -(-3 * per_device // sites.shape[1])
-        cap = -(-cap // 16) * 16
+        cap = -(-cap // 8) * 8
         return jax.shard_map(
             functools.partial(local, (sector_size, section_size // owners, owners, cap)),
             mesh=split,

time: 141 us -> 128 us (0.908)
  Pallas kernels: 133 us -> 124 us
  local copies, waits for them, and re-layouts: 6.33 us -> 3.05 us
    pallas_call x1, Pallas kernels: 133 us -> 124 us  [local(): pl.pallas_call(functools.partial(kernel, sizes), out_shape=(jax.ShapeDtyp...]
    unnamed x3 -> x2, local copies, waits for them, and re-layouts: 4.78 us -> 3.05 us
    pallas_call x1 -> x0, local copies, waits for them, and re-layouts: 1.56 us -> none  [local(): pl.pallas_call(functools.partial(kernel, sizes), out_shape=(jax.ShapeDtyp...]
where the time goes in v3:
time: 128 us
  Pallas kernels  124 us (97%)
  local copies, waits for them, and re-layouts  3.05 us (2%)
    pallas_call x1, Pallas kernels, local(): pl.pallas_call(functools.partial(kernel, sizes), out_shape=(jax.ShapeDtyp...  124 us
    unnamed x2, local copies, waits for them, and re-layouts  3.05 us

profile of v3, /device:TPU:0, one launch (start us, length us, event | category | flops | bytes accessed | tf_op | source)
XLA Modules:
  0.0 128.1 jit_solution(4625325202149278128)
XLA Ops:
  0.6 124.4 %shard_map.68 = (bf16[8,384]{1,0:T(8,128)(2,1)}, bf16[384,512]{1,0:T(8,128)(2,1)}) custom-call(bf16[384,512]{1,0:T(8,128)(2,1)} %vec_ref.1, s32[2,384]{1,0:T(2,128)} %bitcast.4, s32[2,384]{1,0:T(2,128)} %bitcast.5, bf16[2,4,512,2048]{3,2,1,0:T(8,128)(2,1)} %site_ref.1, bf16[2,4,4,64,512]{4,3,2,1,0:T(8,128)(2,1)} %env_ref.1), custom_call_target="tpu_custom_call" | custom-call | tf_op jit(solution)/shard_map/pallas_call | solution.py:402
  125.0 1.3 %copy.9 = bf16[384,8]{0,1:T(8,128)(2,1)} copy(bf16[384,8]{0,1:T(8,128)(2,1)} %bitcast.3) | data formatting | bytes 12288
  126.3 1.8 %copy.10 = bf16[384,512]{1,0:T(8,128)(2,1)} copy(bf16[384,512]{1,0:T(8,128)(2,1)} %get-tuple-element.9) | data formatting | bytes 786432

commit v4 on v3

--- a/solution.py
+++ b/solution.py
@@ -74,21 +74,24 @@
     loop(1, n, greet)
     loop(0, (n_grp - 1) * n_own, greet_far)
 
+    def far(block, home):
+        side = jnp.where(home < blocks // 2, block > home, block < home)
+        return 2 * jnp.maximum(block - home, home - block) + jnp.where(side, 1, 0)
+
+    def sends(block, c, home):
+        return far(block, home) <= far(c, home)
+
+    my_block = lax.div(row_me, per_block)
+
     def env_part(k, origin, t):
-        column = lax.rem(lax.div(origin, per_block) + t, blocks) * LANES
         return env_in.at[
-            k, :, pl.ds(pl.multiple_of(origin * depth, depth), depth), pl.ds(pl.multiple_of(column, LANES), LANES)
+            k, :, pl.ds(pl.multiple_of(origin * depth, depth), depth), pl.ds(t * LANES, LANES)
         ]
-
-    def has_third(origin):
-        m = lax.div(origin, per_block)
-        return jnp.logical_or(m == 0, m == blocks - 1)
 
     def env_copy(k, d, t):
         target = row_peer(row_me + d)
-        column = lax.rem(lax.div(row_me, per_block) + t, blocks) * LANES
-        return pltpu.make_async_remote_copy(
-            src_ref=env_ref.at[k, target[2], :, :, pl.ds(pl.multiple_of(column, LANES), LANES)],
+        return pltpu.make_async_remote_copy(
+            src_ref=env_ref.at[k, target[2], :, :, pl.ds(t * LANES, LANES)],
             dst_ref=env_part(k, row_me, t),
             send_sem=esend.at[k, d, t],
             recv_sem=erecv.at[k, d, t],
@@ -96,17 +99,15 @@
             device_id_type=MESH,
         )
 
-    def env_own(k, t):
-        column = lax.rem(lax.div(row_me, per_block) + t, blocks) * LANES
+    def env_own(k):
         return pltpu.make_async_copy(
-            env_ref.at[k, oi, :, :, pl.ds(pl.multiple_of(column, LANES), LANES)],
-            env_part(k, row_me, t),
-            erecv.at[k, 0, t],
+            env_ref.at[k, oi],
+            env_in.at[k, :, pl.ds(pl.multiple_of(row_me * depth, depth), depth), :],
+            erecv.at[k, 0, 0],
         )
 
     def env_arrival(k, d, t):
-        origin = lax.rem(row_me - d + n_row, n_row)
-        part = env_part(k, origin, t)
+        part = env_part(k, lax.rem(row_me - d + n_row, n_row), t)
         return pltpu.make_async_remote_copy(
             src_ref=part,
             dst_ref=part,
@@ -116,60 +117,36 @@
             device_id_type=MESH,
         )
 
+    def for_sent(d, act):
+        home = lax.div(lax.rem(row_me + d, n_row), per_block)
+        for t in range(blocks):
+            pl.when(sends(my_block, t, home))(functools.partial(act, d, t))
+
+    def for_arriving(d, act):
+        origin = lax.div(lax.rem(row_me - d + n_row, n_row), per_block)
+        for t in range(blocks):
+            pl.when(sends(origin, t, my_block))(functools.partial(act, d, t))
+
     def env_start(k):
-        def one(d):
-            env_copy(k, d, 0).start()
-            env_copy(k, d, 1).start()
-
-            @pl.when(has_third(row_me))
-            def _():
-                env_copy(k, d, 2).start()
-
-        env_own(k, 0).start()
-        env_own(k, 1).start()
-
-        @pl.when(has_third(row_me))
-        def _():
-            env_own(k, 2).start()
-
-        loop(1, n_row, one)
+        env_own(k).start()
+        loop(1, n_row, lambda d: for_sent(d, lambda d, t: env_copy(k, d, t).start()))
 
     def env_wait(k):
-        def one(d):
-            env_arrival(k, d, 0).wait_recv()
-            env_arrival(k, d, 1).wait_recv()
-
-            @pl.when(has_third(lax.rem(row_me - d + n_row, n_row)))
-            def _():
-                env_arrival(k, d, 2).wait_recv()
-
-        env_own(k, 0).wait()
-        env_own(k, 1).wait()
-
-        @pl.when(has_third(row_me))
-        def _():
-            env_own(k, 2).wait()
-
-        loop(1, n_row, one)
+        env_own(k).wait()
+        loop(1, n_row, lambda d: for_arriving(d, lambda d, t: env_arrival(k, d, t).wait_recv()))
 
     def env_sent(k):
-        def one(d):
-            env_copy(k, d, 0).wait_send()
-            env_copy(k, d, 1).wait_send()
-
-            @pl.when(has_third(row_me))
-            def _():
-                env_copy(k, d, 2).wait_send()
-
-        loop(1, n_row, one)
+        loop(1, n_row, lambda d: for_sent(d, lambda d, t: env_copy(k, d, t).wait_send()))
 
     def env_build(k):
         for m in range(blocks):
-            for t in range(3 if m in (0, blocks - 1) else 2):
-                c = (m + t) % blocks
-                at = (slice(m * LANES, (m + 1) * LANES), slice(c * LANES, (c + 1) * LANES))
-                part = env_in[k, :, at[0], at[1]]
-                env_w[:, at[0], at[1]] = part if t == 0 else part + part
+            for c in range(blocks):
+
+                @pl.when(sends(m, c, my_block))
+                def _(m=m, c=c):
+                    at = (slice(m * LANES, (m + 1) * LANES), slice(c * LANES, (c + 1) * LANES))
+                    part = env_in[k, :, at[0], at[1]]
+                    env_w[:, at[0], at[1]] = part if m == c else part + part
 
     def relative(labels):
         shifted = labels - me
@@ -395,6 +372,7 @@
     n, n_row = n_sec * n_own, n_grp * n_own
     samples, width = vectors.shape
     slots = n * cap
+    blocks = width // LANES
     vmem = pl.BlockSpec(memory_space=pltpu.VMEM)
     hbm = pl.BlockSpec(memory_space=pl.ANY)
     dma = pltpu.SemaphoreType.DMA
@@ -417,7 +395,7 @@
             pltpu.VMEM((ORBITALS, samples, n * LANES), BF16),
             dma((ORBITALS,)),
             dma((ORBITALS, n)), dma((ORBITALS, n)), dma((ORBITALS, n)), dma((ORBITALS, n)),
-            dma((ORBITALS, n_row, 3)), dma((ORBITALS, n_row, 3)),
+            dma((ORBITALS, n_row, blocks)), dma((ORBITALS, n_row, blocks)),
             dma((n,)), dma((n,)), dma((n,)), dma((n,)),
         ],
         compiler_params=pltpu.CompilerParams(

time: 128 us -> 112 us (0.88)
  Pallas kernels: 124 us -> 108 us
    pallas_call x1, Pallas kernels: 124 us -> 108 us  [local(): pl.pallas_call(functools.partial(kernel, sizes), out_shape=(jax.ShapeDtyp...]
where the time goes in v4:
time: 112 us
  Pallas kernels  108 us (96%)
  local copies, waits for them, and re-layouts  3.05 us (3%)
    pallas_call x1, Pallas kernels, local(): pl.pallas_call(functools.partial(kernel, sizes), out_shape=(jax.ShapeDtyp...  108 us
    unnamed x2, local copies, waits for them, and re-layouts  3.05 us

profile of v4, /device:TPU:0, one launch (start us, length us, event | category | flops | bytes accessed | tf_op | source)
XLA Modules:
  0.0 112.0 jit_solution(15783940404868321278)
XLA Ops:
  0.6 108.4 %shard_map.68 = (bf16[8,384]{1,0:T(8,128)(2,1)}, bf16[384,512]{1,0:T(8,128)(2,1)}) custom-call(bf16[384,512]{1,0:T(8,128)(2,1)} %vec_ref.1, s32[2,384]{1,0:T(2,128)} %bitcast.4, s32[2,384]{1,0:T(2,128)} %bitcast.5, bf16[2,4,512,2048]{3,2,1,0:T(8,128)(2,1)} %site_ref.1, bf16[2,4,4,64,512]{4,3,2,1,0:T(8,128)(2,1)} %env_ref.1), custom_call_target="tpu_custom_call" | custom-call | tf_op jit(solution)/shard_map/pallas_call | solution.py:380
  109.0 1.3 %copy.9 = bf16[384,8]{0,1:T(8,128)(2,1)} copy(bf16[384,8]{0,1:T(8,128)(2,1)} %bitcast.3) | data formatting | bytes 12288
  110.3 1.8 %copy.10 = bf16[384,512]{1,0:T(8,128)(2,1)} copy(bf16[384,512]{1,0:T(8,128)(2,1)} %get-tuple-element.9) | data formatting | bytes 786432

commit v5 on v4

--- a/solution.py
+++ b/solution.py
@@ -157,9 +157,8 @@
     upper = (first < second).astype(F32).astype(BF16)
     slot_rows = []
     slot_columns = []
-    marks = jnp.zeros((MARKS, n * LANES), F32)
     mark_row = lax.broadcasted_iota(jnp.int32, (MARKS, samples), 0)
-    slot_lane = lax.broadcasted_iota(jnp.int32, (samples, n * LANES), 1).astype(F32)
+    wide_columns = []
     for k in range(ORBITALS):
         label = relative(sec_ref[k : k + 1, :])
         hot = (lax.broadcasted_iota(jnp.int32, (n, samples), 0).astype(F32) == label).astype(F32)
@@ -169,10 +168,19 @@
         columns = [jnp.sum(jnp.where(first == second, row, 0.0), axis=1, keepdims=True) for row in both]
         slot_rows.append(both[0])
         slot_columns.append(columns[0])
-        hot_t[k] = (slot_lane == columns[1]).astype(F32).astype(BF16)
-        mark = (mark_row == out_ref[k : k + 1, :] + OUTCOMES * k).astype(F32).astype(BF16)
-        marks = marks + jnp.dot(mark, hot_t[k], preferred_element_type=F32)
-    mark_s[...] = marks.astype(BF16)
+        wide_columns.append(columns[1])
+
+    def make_marks():
+        marks = jnp.zeros((MARKS, n * LANES), F32)
+        slot_lane = lax.broadcasted_iota(jnp.int32, (samples, n * LANES), 1).astype(F32)
+        for k in range(ORBITALS):
+            hot_t[k] = (slot_lane == wide_columns[k]).astype(F32).astype(BF16)
+            mark = (mark_row == out_ref[k : k + 1, :] + OUTCOMES * k).astype(F32).astype(BF16)
+            marks = marks + jnp.dot(mark, hot_t[k], preferred_element_type=F32)
+        mark_s[...] = marks.astype(BF16)
+
+    pl.semaphore_wait(barrier, n - 1 + (n_grp - 1) * n_own)
+    env_start(0)
 
     row_at = lax.broadcasted_iota(jnp.int32, (rows, per_chunk * LANES), 0)
     lane_at = lax.broadcasted_iota(jnp.int32, (rows, per_chunk * LANES), 1)
@@ -183,9 +191,6 @@
         spread = jnp.where(same, 1.0, spread)
     spread = spread.astype(BF16)
 
-    env_w[...] = jnp.zeros_like(env_w)
-
-    pl.semaphore_wait(barrier, n - 1 + (n_grp - 1) * n_own)
 
     def piece(ref, r):
         return ref.at[pl.ds(pl.multiple_of(r * 2 * cap, 16), 2 * cap)]
@@ -312,7 +317,8 @@
         loop(0, CHUNKS, pack)
         fr[k][: 2 * cap] = fs[k][: 2 * cap]
         if k == 0:
-            env_start(0)
+            env_w[...] = jnp.zeros_like(env_w)
+            make_marks()
             loop(1, n, lambda r: mark_copy(r).start())
             mark_r[:, :LANES] = mark_s[:, :LANES]
         site_copies[k].wait()

time: 112 us -> 113 us (level)
  no operation moved by 1% of the time
where the time goes in v5:
time: 113 us; the launch traced here: 112 us
  Pallas kernels  109 us (96%)
  local copies, waits for them, and re-layouts  3.05 us (3%)
    pallas_call x1, Pallas kernels, local(): pl.pallas_call(functools.partial(kernel, sizes), out_shape=(jax.ShapeDtyp...  109 us
    unnamed x2, local copies, waits for them, and re-layouts  3.05 us

profile of v5, /device:TPU:0, one launch (start us, length us, event | category | flops | bytes accessed | tf_op | source)
XLA Modules:
  0.0 112.4 jit_solution(2371170059123766209)
XLA Ops:
  0.6 108.7 %shard_map.68 = (bf16[8,384]{1,0:T(8,128)(2,1)}, bf16[384,512]{1,0:T(8,128)(2,1)}) custom-call(bf16[384,512]{1,0:T(8,128)(2,1)} %vec_ref.1, s32[2,384]{1,0:T(2,128)} %bitcast.4, s32[2,384]{1,0:T(2,128)} %bitcast.5, bf16[2,4,512,2048]{3,2,1,0:T(8,128)(2,1)} %site_ref.1, bf16[2,4,4,64,512]{4,3,2,1,0:T(8,128)(2,1)} %env_ref.1), custom_call_target="tpu_custom_call" | custom-call | tf_op jit(solution)/shard_map/pallas_call | solution.py:386
  109.3 1.3 %copy.9 = bf16[384,8]{0,1:T(8,128)(2,1)} copy(bf16[384,8]{0,1:T(8,128)(2,1)} %bitcast.3) | data formatting | bytes 12288
  110.6 1.8 %copy.10 = bf16[384,512]{1,0:T(8,128)(2,1)} copy(bf16[384,512]{1,0:T(8,128)(2,1)} %get-tuple-element.9) | data formatting | bytes 786432

commit v6 on v5

--- a/solution.py
+++ b/solution.py
@@ -338,15 +338,14 @@
             branch(k, c, lambda s: first_product(k, c, s, left))
 
         if k == 0:
-            loop(0, CHUNKS, lead)
+            loop(0, CHUNKS // 2, lead)
             loop(1, n, lambda r: mark_copy(r).wait_recv())
         env_wait(k)
         env_build(k)
         if k == 0:
             env_start(1)
-            loop(0, CHUNKS, rest)
-        else:
-            loop(0, CHUNKS, work)
+            loop(0, CHUNKS // 2, rest)
+        loop(CHUNKS // 2 if k == 0 else 0, CHUNKS, work)
         rr[k][: 2 * cap] = rs[k][: 2 * cap]
 
         def gather(c, total, k=k):

time: 113 us -> 112 us (level)
  no operation moved by 1% of the time
where the time goes in v6:
time: 112 us
  Pallas kernels  108 us (96%)
  local copies, waits for them, and re-layouts  3.05 us (3%)
    pallas_call x1, Pallas kernels, local(): pl.pallas_call(functools.partial(kernel, sizes), out_shape=(jax.ShapeDtyp...  108 us
    unnamed x2, local copies, waits for them, and re-layouts  3.05 us

profile of v6, /device:TPU:0, one launch (start us, length us, event | category | flops | bytes accessed | tf_op | source)
XLA Modules:
  0.0 112.0 jit_solution(9024344570533452586)
XLA Ops:
  0.6 108.3 %shard_map.68 = (bf16[8,384]{1,0:T(8,128)(2,1)}, bf16[384,512]{1,0:T(8,128)(2,1)}) custom-call(bf16[384,512]{1,0:T(8,128)(2,1)} %vec_ref.1, s32[2,384]{1,0:T(2,128)} %bitcast.4, s32[2,384]{1,0:T(2,128)} %bitcast.5, bf16[2,4,512,2048]{3,2,1,0:T(8,128)(2,1)} %site_ref.1, bf16[2,4,4,64,512]{4,3,2,1,0:T(8,128)(2,1)} %env_ref.1), custom_call_target="tpu_custom_call" | custom-call | tf_op jit(solution)/shard_map/pallas_call | solution.py:385
  108.9 1.3 %copy.9 = bf16[384,8]{0,1:T(8,128)(2,1)} copy(bf16[384,8]{0,1:T(8,128)(2,1)} %bitcast.3) | data formatting | bytes 12288
  110.2 1.8 %copy.10 = bf16[384,512]{1,0:T(8,128)(2,1)} copy(bf16[384,512]{1,0:T(8,128)(2,1)} %get-tuple-element.9) | data formatting | bytes 786432
